TPU v7x, 128 devices: a whole 4x4x4 slice. The times are simulated.
128 devices in a mesh: slab: 64 (over x, z_lo, y, core), patch: 2 (over z_hi).
Axes of the slice: x: 4, y: 4, z: 4 (z_hi: 2, z_lo: 2; z = z_hi * 2 + z_lo), core: 2. Of those that a mesh axis runs over, the one named last changes fastest.
Arguments:
- coarse_phi: float32 [1024, 128, 128], P(('slab', 'patch')), may hold values from -6 to 6
- coarse_rho: float32 [1024, 128, 128], P(('slab', 'patch')), may hold values from -6 to 6
- fine_patch_potential: float32 [256, 64, 4096], P(('slab', 'patch')), may hold values from -6 to 6
- fine_patch_source: float32 [256, 64, 4096], P(('slab', 'patch')), may hold values from -96 to 96
- anchors: int32 [256, 2], P('slab'), may hold values from 1 to 111
- owned_count: int32 [128], P('slab'), may hold values from 0 to 2, as said below
- colour_order: int32 [4], replicated, may hold values from 0 to 1
Outputs:
- coarse_out: float32 [1024, 128, 128], P(('slab', 'patch'))
- patch_out: float32 [256, 64, 4096], P(('slab', 'patch'))
Inputs may be any that keep to these rules, and one draw needn't show every extreme that they name: A device's live patches are its first owned_count slots; the two devices of one slab group (indices 2 g and 2 g + 1) hold at most 2 live patches together, and some group holds exactly 2. `anchors`: every region and the layer of cells around it lie inside the grid in x and y.
All inputs are finite; a program needn't handle non-finite values.
Results may differ from a plain program's by a relative error of at most 0.0003.
Values sent between devices are 32-bit elements; how exact they have to be, the bound alone decides.
A program may use at most 192 MiB of HBM per device.

v0:
```python
import jax
import jax.numpy as jnp
from jax import lax
from jax.sharding import PartitionSpec as P

PATCH_FINE = 64
RATIO = 4
SWEEPS = 4
PATCH_COARSE = 16


accel_scale = 1.0


def swapped(value, axis, apart):
    mask = 2**apart
    pairs = [(source, source ^ mask) for source in range(lax.axis_size(axis))]
    return lax.ppermute(value, axis, pairs)


def padded_2(cells, sides, width):
    for axis, dim in sides:
        count = lax.axis_size(axis)
        ends = count - 1
        head = lax.slice_in_dim(cells, 0, width, axis=dim)
        tail = lax.slice_in_dim(cells, cells.shape[dim] - width, cells.shape[dim], axis=dim)
        cells = jnp.concatenate(
            [
                lax.ppermute(tail, axis, [(i, (i + 1) % count) for i in range(ends)]),
                cells,
                lax.ppermute(head, axis, [((i + 1) % count, i) for i in range(ends)]),
            ],
            axis=dim,
        )
    return cells


def int_starts(*values):
    return tuple((jnp.asarray(value).astype(jnp.int32) for value in values))


def face_weight(near_value, center, inverse_step):
    return 1.0 + 1.0 / (1.0 + inverse_step * jnp.abs(near_value - center) / accel_scale)


def relax(center, neighbours, source, inverse_step, step_square, update):
    weight_sum = jnp.zeros_like(center)
    weighted = jnp.zeros_like(center)
    for near_value in neighbours:
        weight = face_weight(near_value, center, inverse_step)
        weight_sum = weight_sum + weight
        weighted = weighted + weight * near_value
    relaxed = (weighted - step_square * source) / weight_sum
    return jnp.where(update, relaxed, center)


def coarse_colour(padded, source, update):
    framed = jnp.pad(padded, ((0, 0), (1, 1), (1, 1)))
    center = framed[1:-1, 1:-1, 1:-1]
    neighbours = [
        framed[:-2, 1:-1, 1:-1],
        framed[2:, 1:-1, 1:-1],
        framed[1:-1, :-2, 1:-1],
        framed[1:-1, 2:, 1:-1],
        framed[1:-1, 1:-1, :-2],
        framed[1:-1, 1:-1, 2:],
    ]
    return relax(center, neighbours, source, 1.0, 1.0, update)


def parity_mask(z_values, extent, colour):
    across = jnp.arange(extent, dtype=jnp.int32)
    plane_sum = across[:, None] + across[None, :]
    return (z_values[:, None, None] + plane_sum[None]) % 2 == colour


def expand(face):
    return jnp.repeat(jnp.repeat(face, RATIO, axis=0), RATIO, axis=1)


def on_device(
    coarse_phi,
    coarse_rho,
    fine_patch_potential,
    fine_patch_source,
    anchors,
    owned_count,
    colour_order,
):
    planes = coarse_phi.shape[0]
    extent = coarse_phi.shape[2]
    slot_total = fine_patch_potential.shape[0]
    own_index = lax.axis_index("patch")
    local_z = jnp.arange(planes, dtype=jnp.int32)
    shell_list = []
    coarse_field = coarse_phi

    def with_rims(field_now):
        return padded_2(field_now, ((("slab", "patch"), 0),), 1)

    for sweep_index in range(SWEEPS):
        first_colour = colour_order[sweep_index]
        padded = with_rims(coarse_field)

        def single_cut(anchor):
            x_anchor = anchor[0]
            y_anchor = anchor[1]
            x_low = lax.dynamic_slice(
                padded, int_starts(1, y_anchor, x_anchor - 1), (planes, PATCH_COARSE, 1)
            )
            x_high = lax.dynamic_slice(
                padded, int_starts(1, y_anchor, x_anchor + PATCH_COARSE), (planes, PATCH_COARSE, 1)
            )
            y_low = lax.dynamic_slice(
                padded, int_starts(1, y_anchor - 1, x_anchor), (planes, 1, PATCH_COARSE)
            )
            y_high = lax.dynamic_slice(
                padded, int_starts(1, y_anchor + PATCH_COARSE, x_anchor), (planes, 1, PATCH_COARSE)
            )
            face_row = jnp.where(own_index == 0, 1 - 1, planes + 1)
            z_face = lax.dynamic_slice(
                padded, int_starts(face_row, y_anchor, x_anchor), (1, PATCH_COARSE, PATCH_COARSE)
            )
            return jnp.concatenate(
                [
                    x_low.reshape(-1),
                    x_high.reshape(-1),
                    y_low.reshape(-1),
                    y_high.reshape(-1),
                    z_face.reshape(-1),
                ]
            )

        own_half = jax.vmap(single_cut)(anchors)
        partner = swapped(own_half, "patch", 0)
        low_half = jnp.where(own_index == 0, own_half, partner)
        high_half = jnp.where(own_index == 0, partner, own_half)
        cycle_size = 4 * planes * PATCH_COARSE
        cycle_low = low_half[:, :cycle_size].reshape(-1, 4, planes, PATCH_COARSE)
        cycle_high = high_half[:, :cycle_size].reshape(-1, 4, planes, PATCH_COARSE)
        cycle_part = jnp.concatenate([cycle_low, cycle_high], axis=2)
        under_face = low_half[:, cycle_size:].reshape(-1, 1, PATCH_COARSE, PATCH_COARSE)
        above_face = high_half[:, cycle_size:].reshape(-1, 1, PATCH_COARSE, PATCH_COARSE)
        shell_list.append(jnp.concatenate([cycle_part, under_face, above_face], axis=1))
        coarse_field = coarse_colour(padded, coarse_rho, parity_mask(local_z, extent, first_colour))
        second_padded = with_rims(coarse_field)
        coarse_field = coarse_colour(
            second_padded, coarse_rho, parity_mask(local_z, extent, 1 - first_colour)
        )
    shells = jnp.stack(shell_list)
    z_fine = jnp.arange(PATCH_FINE, dtype=jnp.int32)[:, None]
    flat_index = jnp.arange(PATCH_FINE * PATCH_FINE, dtype=jnp.int32)[None, :]
    y_fine = flat_index // PATCH_FINE
    x_fine = flat_index % PATCH_FINE
    fine_parity = (z_fine + y_fine + x_fine) % 2

    def sweep_patch(potential, density, group_slot):
        fine_field = potential
        for sweep_index in range(SWEEPS):
            face_set = shells[sweep_index, group_slot]
            x_low = jnp.repeat(expand(face_set[0]), PATCH_FINE, axis=1)
            x_high = jnp.repeat(expand(face_set[1]), PATCH_FINE, axis=1)
            y_low = jnp.tile(expand(face_set[2]), (1, PATCH_FINE))
            y_high = jnp.tile(expand(face_set[3]), (1, PATCH_FINE))
            under = expand(face_set[4]).reshape(1, PATCH_FINE * PATCH_FINE)
            above = expand(face_set[5]).reshape(1, PATCH_FINE * PATCH_FINE)
            first_colour = colour_order[sweep_index]
            for colour in (first_colour, 1 - first_colour):
                neighbours = [
                    jnp.concatenate([under, fine_field[:-1]], axis=0),
                    jnp.concatenate([fine_field[1:], above], axis=0),
                    jnp.where(y_fine == 0, y_low, jnp.roll(fine_field, PATCH_FINE, axis=1)),
                    jnp.where(
                        y_fine == PATCH_FINE - 1, y_high, jnp.roll(fine_field, -PATCH_FINE, axis=1)
                    ),
                    jnp.where(x_fine == 0, x_low, jnp.roll(fine_field, 1, axis=1)),
                    jnp.where(x_fine == PATCH_FINE - 1, x_high, jnp.roll(fine_field, -1, axis=1)),
                ]
                fine_field = relax(
                    fine_field,
                    neighbours,
                    density,
                    float(RATIO),
                    1.0 / (RATIO * RATIO),
                    fine_parity == colour,
                )
        return fine_field

    own_count = owned_count[own_index]

    def sweep_slot(slot_index, finished):
        group_slot = own_index * slot_total + slot_index
        swept = sweep_patch(
            fine_patch_potential[slot_index], fine_patch_source[slot_index], group_slot
        )
        return lax.dynamic_update_index_in_dim(finished, swept, slot_index, 0)

    patch_out = lax.fori_loop(0, own_count, sweep_slot, fine_patch_potential)
    return (coarse_field, patch_out)


def solution(mesh):
    in_specs = (
        P(("slab", "patch"), None, None),
        P(("slab", "patch"), None, None),
        P(("slab", "patch"), None, None),
        P(("slab", "patch"), None, None),
        P("slab", None),
        P("slab"),
        P(),
    )
    out_specs = (P(("slab", "patch"), None, None), P(("slab", "patch"), None, None))
    return jax.shard_map(
        on_device, mesh=mesh, in_specs=in_specs, out_specs=out_specs, check_vma=False
    )
```

profile of v0, /device:TPU:7, one launch (start us, length us, event | category | flops | bytes accessed | tf_op | source)
XLA Modules:
  0.0 911.7 jit_solution(13532242000333917969)
XLA Ops:
  20.5 10.5 %while.38 = (s32[]{:T(128)}, f32[10,128,128]{2,1,0:T(8,128)S(1)}, s32[4,3]{1,0:T(4,128)S(1)}, f32[4,1,16,16]{3,2,1,0:T(8,128)S(1)}, s32[]{:T(128)}) while((s32[]{:T(128)}, f32[10,128,128]{2,1,0:T(8,128)S(1)}, s32[4,3]{1,0:T(4,128)S(1)}, f32[4,1,16,16]{3,2,1,0:T(8,128)S(1)}, s32[]{:T(128)}) %tuple.708), condition=%wide.while_cond.4, body=%wide.while_body.4.sunk | while | flops 2 | bytes 16521 | solution.py:121
  40.4 12.9 %while.37 = (s32[]{:T(128)}, f32[10,128,128]{2,0,1:T(8,128)}, s32[4,3]{1,0:T(4,128)S(1)}, f32[4,8,1,16]{3,1,2,0:T(8,128)S(1)}, s32[]{:T(128)}) while((s32[]{:T(128)}, f32[10,128,128]{2,0,1:T(8,128)}, s32[4,3]{1,0:T(4,128)S(1)}, f32[4,8,1,16]{3,1,2,0:T(8,128)S(1)}, s32[]{:T(128)}) %tuple.705), condition=%wide.while_cond.3, body=%wide.while_body.3.sunk | while | flops 2 | bytes 4745 | solution.py:117
  53.4 12.6 %while.36 = (s32[]{:T(128)}, f32[10,128,128]{2,0,1:T(8,128)}, s32[4,3]{1,0:T(4,128)S(1)}, f32[4,8,1,16]{3,1,2,0:T(8,128)S(1)}, s32[]{:T(128)}) while((s32[]{:T(128)}, f32[10,128,128]{2,0,1:T(8,128)}, s32[4,3]{1,0:T(4,128)S(1)}, f32[4,8,1,16]{3,1,2,0:T(8,128)S(1)}, s32[]{:T(128)}) %tuple.720), condition=%wide.while_cond.2, body=%wide.while_body.2.sunk | while | flops 2 | bytes 4745 | solution.py:114
  66.1 10.1 %while.35 = (s32[]{:T(128)}, f32[10,128,128]{1,0,2:T(8,128)S(1)}, s32[4,3]{1,0:T(4,128)S(1)}, f32[4,8,16,1]{2,1,3,0:T(8,128)S(1)}, s32[]{:T(128)}) while((s32[]{:T(128)}, f32[10,128,128]{1,0,2:T(8,128)S(1)}, s32[4,3]{1,0:T(4,128)S(1)}, f32[4,8,16,1]{2,1,3,0:T(8,128)S(1)}, s32[]{:T(128)}) %tuple.699), condition=%wide.while_cond.1, body=%wide.while_body.1.sunk | while | flops 2 | bytes 8329 | solution.py:111
  76.2 10.5 %while.34 = (s32[]{:T(128)}, f32[10,128,128]{1,0,2:T(8,128)S(1)}, s32[4,3]{1,0:T(4,128)S(1)}, f32[4,8,16,1]{2,1,3,0:T(8,128)S(1)}, s32[]{:T(128)}) while((s32[]{:T(128)}, f32[10,128,128]{1,0,2:T(8,128)S(1)}, s32[4,3]{1,0:T(4,128)S(1)}, f32[4,8,16,1]{2,1,3,0:T(8,128)S(1)}, s32[]{:T(128)}) %tuple.715), condition=%wide.while_cond, body=%wide.while_body.sunk | while | flops 2 | bytes 8329 | solution.py:108
  102.6 10.9 %while.43 = (s32[]{:T(128)}, f32[10,128,128]{2,1,0:T(8,128)S(1)}, s32[4,3]{1,0:T(4,128)S(1)}, f32[4,1,16,16]{3,2,1,0:T(8,128)S(1)}, s32[]{:T(128)}) while((s32[]{:T(128)}, f32[10,128,128]{2,1,0:T(8,128)S(1)}, s32[4,3]{1,0:T(4,128)S(1)}, f32[4,1,16,16]{3,2,1,0:T(8,128)S(1)}, s32[]{:T(128)}) %tuple.736), condition=%wide.while_cond.9, body=%wide.while_body.9.sunk | while | flops 2 | bytes 16521 | solution.py:121
  113.6 12.8 %while.42 = (s32[]{:T(128)}, f32[10,128,128]{2,0,1:T(8,128)}, s32[4,3]{1,0:T(4,128)S(1)}, f32[4,8,1,16]{3,1,2,0:T(8,128)S(1)}, s32[]{:T(128)}) while((s32[]{:T(128)}, f32[10,128,128]{2,0,1:T(8,128)}, s32[4,3]{1,0:T(4,128)S(1)}, f32[4,8,1,16]{3,1,2,0:T(8,128)S(1)}, s32[]{:T(128)}) %tuple.733), condition=%wide.while_cond.8, body=%wide.while_body.8.sunk | while | flops 2 | bytes 4745 | solution.py:117
  126.5 12.8 %while.41 = (s32[]{:T(128)}, f32[10,128,128]{2,0,1:T(8,128)}, s32[4,3]{1,0:T(4,128)S(1)}, f32[4,8,1,16]{3,1,2,0:T(8,128)S(1)}, s32[]{:T(128)}) while((s32[]{:T(128)}, f32[10,128,128]{2,0,1:T(8,128)}, s32[4,3]{1,0:T(4,128)S(1)}, f32[4,8,1,16]{3,1,2,0:T(8,128)S(1)}, s32[]{:T(128)}) %tuple.730), condition=%wide.while_cond.7, body=%wide.while_body.7.sunk | while | flops 2 | bytes 4745 | solution.py:114
  139.4 10.7 %while.40 = (s32[]{:T(128)}, f32[10,128,128]{1,0,2:T(8,128)S(1)}, s32[4,3]{1,0:T(4,128)S(1)}, f32[4,8,16,1]{2,1,3,0:T(8,128)S(1)}, s32[]{:T(128)}) while((s32[]{:T(128)}, f32[10,128,128]{1,0,2:T(8,128)S(1)}, s32[4,3]{1,0:T(4,128)S(1)}, f32[4,8,16,1]{2,1,3,0:T(8,128)S(1)}, s32[]{:T(128)}) %tuple.727), condition=%wide.while_cond.6, body=%wide.while_body.6.sunk | while | flops 2 | bytes 8329 | solution.py:111
  150.1 10.8 %while.39 = (s32[]{:T(128)}, f32[10,128,128]{1,0,2:T(8,128)S(1)}, s32[4,3]{1,0:T(4,128)S(1)}, f32[4,8,16,1]{2,1,3,0:T(8,128)S(1)}, s32[]{:T(128)}) while((s32[]{:T(128)}, f32[10,128,128]{1,0,2:T(8,128)S(1)}, s32[4,3]{1,0:T(4,128)S(1)}, f32[4,8,16,1]{2,1,3,0:T(8,128)S(1)}, s32[]{:T(128)}) %tuple.724), condition=%wide.while_cond.5, body=%wide.while_body.5.sunk | while | flops 2 | bytes 8329 | solution.py:108
  193.2 11.1 %while.48 = (s32[]{:T(128)}, f32[10,128,128]{2,1,0:T(8,128)S(1)}, s32[4,3]{1,0:T(4,128)S(1)}, f32[4,1,16,16]{3,2,1,0:T(8,128)S(1)}, s32[]{:T(128)}) while((s32[]{:T(128)}, f32[10,128,128]{2,1,0:T(8,128)S(1)}, s32[4,3]{1,0:T(4,128)S(1)}, f32[4,1,16,16]{3,2,1,0:T(8,128)S(1)}, s32[]{:T(128)}) %tuple.737), condition=%wide.while_cond.14, body=%wide.while_body.14.sunk | while | flops 2 | bytes 16521 | solution.py:121
  214.5 13.6 %while.47 = (s32[]{:T(128)}, f32[10,128,128]{2,0,1:T(8,128)}, s32[4,3]{1,0:T(4,128)S(1)}, f32[4,8,1,16]{3,1,2,0:T(8,128)S(1)}, s32[]{:T(128)}) while((s32[]{:T(128)}, f32[10,128,128]{2,0,1:T(8,128)}, s32[4,3]{1,0:T(4,128)S(1)}, f32[4,8,1,16]{3,1,2,0:T(8,128)S(1)}, s32[]{:T(128)}) %tuple.734), condition=%wide.while_cond.13, body=%wide.while_body.13.sunk | while | flops 2 | bytes 4745 | solution.py:117
  228.2 12.9 %while.46 = (s32[]{:T(128)}, f32[10,128,128]{2,0,1:T(8,128)}, s32[4,3]{1,0:T(4,128)S(1)}, f32[4,8,1,16]{3,1,2,0:T(8,128)S(1)}, s32[]{:T(128)}) while((s32[]{:T(128)}, f32[10,128,128]{2,0,1:T(8,128)}, s32[4,3]{1,0:T(4,128)S(1)}, f32[4,8,1,16]{3,1,2,0:T(8,128)S(1)}, s32[]{:T(128)}) %tuple.731), condition=%wide.while_cond.12, body=%wide.while_body.12.sunk | while | flops 2 | bytes 4745 | solution.py:114
  241.2 10.4 %while.45 = (s32[]{:T(128)}, f32[10,128,128]{1,0,2:T(8,128)S(1)}, s32[4,3]{1,0:T(4,128)S(1)}, f32[4,8,16,1]{2,1,3,0:T(8,128)S(1)}, s32[]{:T(128)}) while((s32[]{:T(128)}, f32[10,128,128]{1,0,2:T(8,128)S(1)}, s32[4,3]{1,0:T(4,128)S(1)}, f32[4,8,16,1]{2,1,3,0:T(8,128)S(1)}, s32[]{:T(128)}) %tuple.728), condition=%wide.while_cond.11, body=%wide.while_body.11.sunk | while | flops 2 | bytes 8329 | solution.py:111
  251.6 10.4 %while.44 = (s32[]{:T(128)}, f32[10,128,128]{1,0,2:T(8,128)S(1)}, s32[4,3]{1,0:T(4,128)S(1)}, f32[4,8,16,1]{2,1,3,0:T(8,128)S(1)}, s32[]{:T(128)}) while((s32[]{:T(128)}, f32[10,128,128]{1,0,2:T(8,128)S(1)}, s32[4,3]{1,0:T(4,128)S(1)}, f32[4,8,16,1]{2,1,3,0:T(8,128)S(1)}, s32[]{:T(128)}) %tuple.725), condition=%wide.while_cond.10, body=%wide.while_body.10.sunk | while | flops 2 | bytes 8329 | solution.py:108
  278.3 10.6 %while.53 = (s32[]{:T(128)}, f32[10,128,128]{2,1,0:T(8,128)S(1)}, s32[4,3]{1,0:T(4,128)S(1)}, f32[4,1,16,16]{3,2,1,0:T(8,128)S(1)}, s32[]{:T(128)}) while((s32[]{:T(128)}, f32[10,128,128]{2,1,0:T(8,128)S(1)}, s32[4,3]{1,0:T(4,128)S(1)}, f32[4,1,16,16]{3,2,1,0:T(8,128)S(1)}, s32[]{:T(128)}) %tuple.738), condition=%wide.while_cond.19, body=%wide.while_body.19.sunk | while | flops 2 | bytes 16521 | solution.py:121
  289.0 13.4 %while.52 = (s32[]{:T(128)}, f32[10,128,128]{2,0,1:T(8,128)}, s32[4,3]{1,0:T(4,128)S(1)}, f32[4,8,1,16]{3,1,2,0:T(8,128)S(1)}, s32[]{:T(128)}) while((s32[]{:T(128)}, f32[10,128,128]{2,0,1:T(8,128)}, s32[4,3]{1,0:T(4,128)S(1)}, f32[4,8,1,16]{3,1,2,0:T(8,128)S(1)}, s32[]{:T(128)}) %tuple.735), condition=%wide.while_cond.18, body=%wide.while_body.18.sunk | while | flops 2 | bytes 4745 | solution.py:117
  302.5 13.2 %while.51 = (s32[]{:T(128)}, f32[10,128,128]{2,0,1:T(8,128)}, s32[4,3]{1,0:T(4,128)S(1)}, f32[4,8,1,16]{3,1,2,0:T(8,128)S(1)}, s32[]{:T(128)}) while((s32[]{:T(128)}, f32[10,128,128]{2,0,1:T(8,128)}, s32[4,3]{1,0:T(4,128)S(1)}, f32[4,8,1,16]{3,1,2,0:T(8,128)S(1)}, s32[]{:T(128)}) %tuple.732), condition=%wide.while_cond.17, body=%wide.while_body.17.sunk | while | flops 2 | bytes 4745 | solution.py:114
  315.8 10.7 %while.50 = (s32[]{:T(128)}, f32[10,128,128]{1,0,2:T(8,128)S(1)}, s32[4,3]{1,0:T(4,128)S(1)}, f32[4,8,16,1]{2,1,3,0:T(8,128)S(1)}, s32[]{:T(128)}) while((s32[]{:T(128)}, f32[10,128,128]{1,0,2:T(8,128)S(1)}, s32[4,3]{1,0:T(4,128)S(1)}, f32[4,8,16,1]{2,1,3,0:T(8,128)S(1)}, s32[]{:T(128)}) %tuple.729), condition=%wide.while_cond.16, body=%wide.while_body.16.sunk | while | flops 2 | bytes 8329 | solution.py:111
  326.6 10.7 %while.49 = (s32[]{:T(128)}, f32[10,128,128]{1,0,2:T(8,128)S(1)}, s32[4,3]{1,0:T(4,128)S(1)}, f32[4,8,16,1]{2,1,3,0:T(8,128)S(1)}, s32[]{:T(128)}) while((s32[]{:T(128)}, f32[10,128,128]{1,0,2:T(8,128)S(1)}, s32[4,3]{1,0:T(4,128)S(1)}, f32[4,8,16,1]{2,1,3,0:T(8,128)S(1)}, s32[]{:T(128)}) %tuple.726), condition=%wide.while_cond.15, body=%wide.while_body.15.sunk | while | flops 2 | bytes 8329 | solution.py:108
  346.0 8.9 collective-permute-start.15
  356.8 549.8 %while.54 = (s32[]{:T(128)}, f32[2,64,4096]{2,1,0:T(8,128)}, s32[]{:T(128)}, s32[]{:T(128)}, s32[]{:T(128)}, /*index=5*/f32[4,4,6,16,16]{4,3,2,1,0:T(8,128)}, s3...) while((s32[]{:T(128)}, f32[2,64,4096]{2,1,0:T(8,128)}, ...), condition=%wide.region_1.2_spmd.clone.clone, body=%wide.region_0.1_spmd.clone.clone.sunk | while | flops 289013760 | bytes 540034304 | solution.py:198
  590.6 39.1 %select_dynamic-update-slice_fusion.2 = f32[2,64,4096]{2,1,0:T(8,128)} fusion(f32[2,64,4096]{2,1,0:T(8,128)} %get-tuple-element.2790, s32[]{:T(128)S(6)} %select_n.1627, f32[1,64,4096]{2,1,0:T(8,128)S(1)} %copy-done.29, f32[1,64,1]{2,1,0:T(8,128)} %get-tuple-element.2388, f32[1,64,4095]{2,1,0:T(8,128)} %get-tuple-element.2389, ...), kind=kLoop, calls=%fused_computation.164.clone.1 | loop fusion | flops 142082048 | bytes 71208448 | tf_op jit(solution)/shard_map/while/body/jit(dynamic_update_index_in_dim)/dynamic_update_slice | solution.py:196
  863.6 39.1 %select_dynamic-update-slice_fusion.2 = f32[2,64,4096]{2,1,0:T(8,128)} fusion(f32[2,64,4096]{2,1,0:T(8,128)} %get-tuple-element.2790, s32[]{:T(128)S(6)} %select_n.1627, f32[1,64,4096]{2,1,0:T(8,128)S(1)} %copy-done.29, f32[1,64,1]{2,1,0:T(8,128)} %get-tuple-element.2388, f32[1,64,4095]{2,1,0:T(8,128)} %get-tuple-element.2389, ...), kind=kLoop, calls=%fused_computation.164.clone.1 | loop fusion | flops 142082048 | bytes 71208448 | tf_op jit(solution)/shard_map/while/body/jit(dynamic_update_index_in_dim)/dynamic_update_slice | solution.py:196
  (1031 shorter events, 812.1 us)
Async XLA Ops:
  1.5 17.0 %collective-permute-start = (f32[1,128,128]{2,1,0:T(8,128)S(1)}, f32[1,128,128]{2,1,0:T(8,128)S(1)}, u32[]{:S(2)}, u32[]{:S(2)}) collective-permute-start(f32[1,128,128]{2,1,0:T(8,128)S(1)} %get-tuple-element.1373), channel_id=1, source_target_pairs={{0,1},{1,2},{2,3},{3,4},{4,5},{5,6},{6,7},{7,8},{8,9},{9,10},{10,1... | collective-permute-start | bytes 196616 | tf_op jit(solution)/shard_map/ppermute | solution.py:29
  7.0 11.6 %collective-permute-start.1 = (f32[1,128,128]{2,1,0:T(8,128)S(1)}, f32[1,128,128]{2,1,0:T(8,128)S(1)}, u32[]{:S(2)}, u32[]{:S(2)}) collective-permute-start(f32[1,128,128]{2,1,0:T(8,128)S(1)} %get-tuple-element.1374), channel_id=1, source_target_pairs={{1,0},{2,1},{3,2},{4,3},{5,4},{6,5},{7,6},{8,7},{9,8},{10,9},{11,1... | collective-permute-start | bytes 196616 | tf_op jit(solution)/shard_map/ppermute | solution.py:31
  9.5 332.0 %copy-start.43 = (s32[128,128]{1,0:T(8,128)}, s32[128,128]{1,0:T(8,128)S(1)}, u32[]{:S(2)}) copy-start(s32[128,128]{1,0:T(8,128)S(1)} %iota_add_fusion) | copy-start | bytes 196612
  33.0 53.9 %copy-start.38 = (f32[8,128,128]{2,1,0:T(8,128)}, f32[8,128,128]{2,1,0:T(8,128)S(1)}, u32[]{:S(2)}) copy-start(f32[8,128,128]{2,1,0:T(8,128)S(1)} %fusion.181) | copy-start | bytes 1572868
  33.0 53.9 %collective-permute-start.2 = (f32[1,128,128]{2,1,0:T(8,128)S(1)}, f32[1,128,128]{2,1,0:T(8,128)S(1)}, u32[]{:S(2)}, u32[]{:S(2)}) collective-permute-start(f32[1,128,128]{2,1,0:T(8,128)S(1)} %get-tuple-element.1371), channel_id=1, source_target_pairs={{0,1},{1,2},{2,3},{3,4},{4,5},{5,6},{6,7},{7,8},{8,9},{9,10},{10,1... | collective-permute-start | bytes 196616 | tf_op jit(solution)/shard_map/ppermute | solution.py:29
  37.3 49.6 %collective-permute-start.3 = (f32[1,128,128]{2,1,0:T(8,128)S(1)}, f32[1,128,128]{2,1,0:T(8,128)S(1)}, u32[]{:S(2)}, u32[]{:S(2)}) collective-permute-start(f32[1,128,128]{2,1,0:T(8,128)S(1)} %get-tuple-element.1372), channel_id=1, source_target_pairs={{1,0},{2,1},{3,2},{4,3},{5,4},{6,5},{7,6},{8,7},{9,8},{10,9},{11,1... | collective-permute-start | bytes 196616 | tf_op jit(solution)/shard_map/ppermute | solution.py:31
  90.1 9.1 collective-permute-start.4
  93.8 6.9 collective-permute-start.5
  97.5 78.8 %collective-permute-start.16 = (f32[4,768]{1,0:T(4,128)S(1)}, f32[4,768]{1,0:T(4,128)S(1)}, u32[]{:S(2)}, u32[]{:S(2)}) collective-permute-start(f32[4,768]{1,0:T(4,128)S(1)} %constant_dynamic-update-slice_fusion.3), channel_id=1, source_target_pairs={{0,1},{1,0},{2,3},{3,2},{4,5},{5,4},{6,7},{7,6},{8,9},{9,8},{10,11... | collective-permute-start | bytes 36872 | tf_op jit(solution)/shard_map/ppermute | solution.py:18
  161.0 15.2 %collective-permute-start.17 = (f32[4,768]{1,0:T(4,128)S(1)}, f32[4,768]{1,0:T(4,128)S(1)}, u32[]{:S(2)}, u32[]{:S(2)}) collective-permute-start(f32[4,768]{1,0:T(4,128)S(1)} %constant_dynamic-update-slice_fusion.8), channel_id=1, source_target_pairs={{0,1},{1,0},{2,3},{3,2},{4,5},{5,4},{6,7},{7,6},{8,9},{9,8},{10,11... | collective-permute-start | bytes 36872 | tf_op jit(solution)/shard_map/ppermute | solution.py:18
  167.5 10.3 %collective-permute-start.6 = (f32[1,128,128]{2,1,0:T(8,128)S(1)}, f32[1,128,128]{2,1,0:T(8,128)S(1)}, u32[]{:S(2)}, u32[]{:S(2)}) collective-permute-start(f32[1,128,128]{2,1,0:T(8,128)S(1)} %get-tuple-element.1367), channel_id=1, source_target_pairs={{0,1},{1,2},{2,3},{3,4},{4,5},{5,6},{6,7},{7,8},{8,9},{9,10},{10,1... | collective-permute-start | bytes 196616 | tf_op jit(solution)/shard_map/ppermute | solution.py:29
  169.4 8.4 collective-permute-start.7
  180.7 8.6 collective-permute-start.8
  184.6 6.6 collective-permute-start.9
  206.2 55.9 %copy-start.39 = (f32[8,128,128]{2,1,0:T(8,128)}, f32[8,128,128]{2,1,0:T(8,128)S(1)}, u32[]{:S(2)}) copy-start(f32[8,128,128]{2,1,0:T(8,128)S(1)} %fusion.101) | copy-start | bytes 1572868
  206.2 55.9 %collective-permute-start.10 = (f32[1,128,128]{2,1,0:T(8,128)S(1)}, f32[1,128,128]{2,1,0:T(8,128)S(1)}, u32[]{:S(2)}, u32[]{:S(2)}) collective-permute-start(f32[1,128,128]{2,1,0:T(8,128)S(1)} %get-tuple-element.1363), channel_id=1, source_target_pairs={{0,1},{1,2},{2,3},{3,4},{4,5},{5,6},{6,7},{7,8},{8,9},{9,10},{10,1... | collective-permute-start | bytes 196616 | tf_op jit(solution)/shard_map/ppermute | solution.py:29
  212.5 49.6 %collective-permute-start.11 = (f32[1,128,128]{2,1,0:T(8,128)S(1)}, f32[1,128,128]{2,1,0:T(8,128)S(1)}, u32[]{:S(2)}, u32[]{:S(2)}) collective-permute-start(f32[1,128,128]{2,1,0:T(8,128)S(1)} %get-tuple-element.1364), channel_id=1, source_target_pairs={{1,0},{2,1},{3,2},{4,3},{5,4},{6,5},{7,6},{8,7},{9,8},{10,9},{11,1... | collective-permute-start | bytes 196616 | tf_op jit(solution)/shard_map/ppermute | solution.py:31
  265.0 9.9 %collective-permute-start.12 = (f32[1,128,128]{2,1,0:T(8,128)S(1)}, f32[1,128,128]{2,1,0:T(8,128)S(1)}, u32[]{:S(2)}, u32[]{:S(2)}) collective-permute-start(f32[1,128,128]{2,1,0:T(8,128)S(1)} %get-tuple-element.1361), channel_id=1, source_target_pairs={{0,1},{1,2},{2,3},{3,4},{4,5},{5,6},{6,7},{7,8},{8,9},{9,10},{10,1... | collective-permute-start | bytes 196616 | tf_op jit(solution)/shard_map/ppermute | solution.py:29
  269.9 6.5 collective-permute-start.13
  273.6 81.2 %collective-permute-start.18 = (f32[4,768]{1,0:T(4,128)S(1)}, f32[4,768]{1,0:T(4,128)S(1)}, u32[]{:S(2)}, u32[]{:S(2)}) collective-permute-start(f32[4,768]{1,0:T(4,128)S(1)} %constant_dynamic-update-slice_fusion.13), channel_id=1, source_target_pairs={{0,1},{1,0},{2,3},{3,2},{4,5},{5,4},{6,7},{7,6},{8,9},{9,8},{10,11... | collective-permute-start | bytes 36872 | tf_op jit(solution)/shard_map/ppermute | solution.py:18
  337.4 17.5 %collective-permute-start.19 = (f32[4,768]{1,0:T(4,128)S(1)}, f32[4,768]{1,0:T(4,128)S(1)}, u32[]{:S(2)}, u32[]{:S(2)}) collective-permute-start(f32[4,768]{1,0:T(4,128)S(1)} %constant_dynamic-update-slice_fusion.18), channel_id=1, source_target_pairs={{0,1},{1,0},{2,3},{3,2},{4,5},{5,4},{6,7},{7,6},{8,9},{9,8},{10,11... | collective-permute-start | bytes 36872 | tf_op jit(solution)/shard_map/ppermute | solution.py:18
  343.4 12.4 %copy-start.57 = (f32[1,4,6,16,16]{4,3,2,1,0:T(8,128)S(1)}, f32[1,4,6,16,16]{4,3,2,1,0:T(8,128)}, u32[]{:S(2)}) copy-start(f32[1,4,6,16,16]{4,3,2,1,0:T(8,128)} %maximum_bitcast_fusion) | copy-start | bytes 73732
  344.1 562.5 %collective-permute-start.14 = (f32[1,128,128]{2,1,0:T(8,128)}, f32[1,128,128]{2,1,0:T(8,128)}, u32[]{:S(2)}, u32[]{:S(2)}) collective-permute-start(f32[1,128,128]{2,1,0:T(8,128)} %get-tuple-element.1359), channel_id=1, source_target_pairs={{0,1},{1,2},{2,3},{3,4},{4,5},{5,6},{6,7},{7,8},{8,9},{9,10},{10,1... | collective-permute-start | bytes 196616 | tf_op jit(solution)/shard_map/ppermute | solution.py:29
  346.0 560.6 %collective-permute-start.15 = (f32[1,128,128]{2,1,0:T(8,128)}, f32[1,128,128]{2,1,0:T(8,128)}, u32[]{:S(2)}, u32[]{:S(2)}) collective-permute-start(f32[1,128,128]{2,1,0:T(8,128)} %get-tuple-element.1360), channel_id=1, source_target_pairs={{1,0},{2,1},{3,2},{4,3},{5,4},{6,5},{7,6},{8,7},{9,8},{10,9},{11,1... | collective-permute-start | bytes 196616 | tf_op jit(solution)/shard_map/ppermute | solution.py:31
  (101 other events, 434.3 us)
where the time goes:
time: 927 us; the launch traced here: 912 us
  local copies, waits for them, and re-layouts  656 us (71%)
  other arithmetic  159 us (17%)
  starting transfers between devices  78.6 us (8%)
    gather x240, local copies, waits for them, and re-layouts  231 us
    dynamic_update_slice x2, other arithmetic, sweep_slot(): return lax.dynamic_update_index_in_dim(finished, swept, slot_index, 0)  78.3 us
    select_n x22, other arithmetic, relax(): return jnp.where(update, relaxed, center)  72.9 us
    another operation x32, local copies, waits for them, and re-layouts, sweep_patch(): y_high = jnp.tile(expand(face_set[3]), (1, PATCH_FINE))  67.4 us
    another operation x32, local copies, waits for them, and re-layouts, sweep_patch(): y_low = jnp.tile(expand(face_set[2]), (1, PATCH_FINE))  66.5 us
    reshape x16, local copies, waits for them, and re-layouts, sweep_patch(): x_high = jnp.repeat(expand(face_set[1]), PATCH_FINE, axis=1)  47.2 us
    reshape x16, local copies, waits for them, and re-layouts, sweep_patch(): x_low = jnp.repeat(expand(face_set[0]), PATCH_FINE, axis=1)  46.3 us
    ppermute x8, starting transfers between devices, padded_2(): lax.ppermute(head, axis, [((i + 1) % count, i) for i in range(ends)])  34.4 us
  transfers between devices with their start and end apart: 20, of which 3 were waited for; matrix products, arithmetic and copies ran while one was open for 83% of the time, Pallas kernels for 0%

commit v1 on v0

v1 whole, which is shorter than its diff:
```python
import functools

import jax
import jax.numpy as jnp
from jax import lax
from jax.experimental import pallas as pl
from jax.experimental.pallas import tpu as pltpu
from jax.sharding import PartitionSpec as P

MESH = pl.DeviceIdType.MESH
SWEEPS = 4
N = 128
CZ = 8
PAIRS = CZ // 2
SLOTS = 2
FINE = 64
HALF = FINE // 2
WIN = 16
TOP = 8
FULL = N + 8
JB = 8


def relaxed(center, neighbours, source):
    r_sum = rv_sum = v_sum = None
    for value in neighbours:
        r = pl.reciprocal(1.0 + jnp.abs(value - center), approx=True)
        rv = r * value
        r_sum = r if r_sum is None else r_sum + r
        rv_sum = rv if rv_sum is None else rv_sum + rv
        v_sum = value if v_sum is None else v_sum + value
    return (rv_sum + (v_sum - source)) * pl.reciprocal(6.0 + r_sum, approx=True)


def iota(shape, dim):
    return lax.broadcasted_iota(jnp.int32, shape, dim)


def split_dot(rows, onehot):
    high = rows.astype(jnp.bfloat16)
    low = (rows - high.astype(jnp.float32)).astype(jnp.bfloat16)
    return jnp.dot(high, onehot, preferred_element_type=jnp.float32) + jnp.dot(
        low, onehot, preferred_element_type=jnp.float32
    )


def kernel(
    groups,
    anchors, owned, order, phi_hbm, rho_hbm, pot_hbm, src_hbm,
    coarse_hbm, patch_hbm,
    raw_phi, raw_rho, raw_pot, raw_src,
    ca, cb, rho_c, halo_rx, rho_rx, full, w_own, w_send, w_rx, far_rx, zplanes, w_rows,
    pa, pb, src_c, x_face, sx, ey, out_stage,
    in_sem, out_sem, halo_send, halo_recv, rho_send, rho_recv, w_ssem, w_rsem, far_send, far_recv,
):
    g = lax.axis_index("slab")
    p = lax.axis_index("patch")
    has_up = jnp.logical_or(g < groups - 1, p == 0)
    has_dn = jnp.logical_or(g > 0, p == 1)
    far_to_ok = jnp.where(p == 0, g > 0, g < groups - 1)
    far_from_ok = jnp.where(p == 0, g < groups - 1, g > 0)
    wrap = lambda v: lax.rem(v + groups, groups)
    up = (wrap(g + p), 1 - p)
    dn = (wrap(g - 1 + p), 1 - p)
    partner = (g, 1 - p)
    far_to = (wrap(g + 2 * p - 1), p)
    far_from = (wrap(g + 1 - 2 * p), p)

    loads = [
        pltpu.make_async_copy(phi_hbm, raw_phi, in_sem.at[0]),
        pltpu.make_async_copy(rho_hbm, raw_rho, in_sem.at[1]),
    ]
    for load in loads:
        load.start()

    def columns(j):
        return pl.ds(pl.multiple_of(j * N, N), N)

    barrier = pltpu.get_barrier_semaphore()
    greeted = ((up, has_up), (dn, has_dn), (far_to, far_to_ok), (far_from, far_from_ok))
    for device, ok in greeted:
        @pl.when(ok)
        def _(device=device):
            pl.semaphore_signal(barrier, inc=1, device_id=device, device_id_type=MESH)

    def fetch(j, carry):
        for slot in range(SLOTS):
            pltpu.make_async_copy(pot_hbm.at[slot, :, columns(j)], raw_pot.at[slot, j], in_sem.at[2]).start()
            pltpu.make_async_copy(src_hbm.at[slot, :, columns(j)], raw_src.at[slot, j], in_sem.at[3]).start()
        return carry

    lax.fori_loop(0, HALF, fetch, 0)

    rows = pl.ds(TOP, N)
    bufs = (ca, cb)

    def halo_copy(s, b, role, side):
        return pltpu.make_async_remote_copy(
            src_ref=bufs[b].at[role, 1 if side == 0 else PAIRS, rows],
            dst_ref=halo_rx.at[s, role, 1 - side],
            send_sem=halo_send.at[s, role, side],
            recv_sem=halo_recv.at[s, role, 1 - side],
            device_id=dn if side == 0 else up,
            device_id_type=MESH,
        )

    def rho_copy(side):
        return pltpu.make_async_remote_copy(
            src_ref=raw_rho.at[0 if side == 0 else CZ - 1],
            dst_ref=rho_rx.at[1 - side],
            send_sem=rho_send.at[side],
            recv_sem=rho_recv.at[1 - side],
            device_id=dn if side == 0 else up,
            device_id_type=MESH,
        )

    def w_copy(s):
        return pltpu.make_async_remote_copy(
            src_ref=w_send, dst_ref=w_rx.at[s], send_sem=w_ssem, recv_sem=w_rsem.at[s],
            device_id=partner, device_id_type=MESH,
        )

    def far_copy(s):
        return pltpu.make_async_remote_copy(
            src_ref=full.at[pl.ds(p * ((CZ - 1) * FULL), N)],
            dst_ref=far_rx.at[s],
            send_sem=far_send,
            recv_sem=far_recv.at[s],
            device_id=far_to,
            device_id_type=MESH,
        )

    def send_halo(s, b, role):
        for side, ok in ((0, has_dn), (1, has_up)):
            @pl.when(ok)
            def _(side=side):
                halo_copy(s, b, role, side).start()

    plane_parity = (iota((N, N), 0) + iota((N, N), 1)) % 2
    lane_c = iota((N, N), 1)
    lane_p = iota((HALF, N), 1)
    fine_parity = (lane_p // FINE + lane_p) % 2
    x_first = lane_p % FINE == 0
    x_last = lane_p % FINE == FINE - 1
    y_first = lane_p < FINE

    for buf in bufs:
        for role in range(2):
            for i in range(PAIRS + 2):
                buf[role, i, 0:TOP, :] = jnp.zeros((TOP, N), jnp.float32)
                buf[role, i, TOP + N :, :] = jnp.zeros((TOP, N), jnp.float32)

    loads[0].wait()
    for i in range(PAIRS):
        even, odd = raw_phi[2 * i], raw_phi[2 * i + 1]
        ca[0, i + 1, rows, :] = jnp.where(plane_parity == 0, even, odd)
        ca[1, i + 1, rows, :] = jnp.where(plane_parity == 0, odd, even)

    pl.semaphore_wait(barrier, sum(ok.astype(jnp.int32) for _, ok in greeted))

    send_halo(0, 0, 0)
    send_halo(0, 0, 1)
    loads[1].wait()
    for side, ok in ((0, has_dn), (1, has_up)):
        @pl.when(ok)
        def _(side=side):
            rho_copy(side).start()

    def extract(s, b, role0_colour):
        for i in range(PAIRS):
            first, second = bufs[b][0, i + 1, rows, :], bufs[b][1, i + 1, rows, :]
            here = plane_parity == role0_colour
            full[pl.ds(2 * i * FULL, N), :] = jnp.where(here, first, second)
            full[pl.ds((2 * i + 1) * FULL, N), :] = jnp.where(here, second, first)

        @pl.when(far_to_ok)
        def _():
            far_copy(s).start()

        lane = iota((CZ, N), 1)
        for whose, dst in ((1 - p, w_send), (p, w_own)):
            packed = jnp.zeros((CZ, N), jnp.float32)
            for k in range(SLOTS):
                ox = anchors[0, whose * SLOTS + k]
                oy = jnp.maximum(anchors[1, whose * SLOTS + k], 1)
                base = k * FINE
                for t in range(WIN):
                    line = full[pl.ds(oy + t, CZ, stride=FULL), :]
                    low = pltpu.roll(line, lax.rem(base + t - (ox - 1) + 2 * N, N), 1)
                    high = pltpu.roll(line, lax.rem(base + WIN + t - (ox + WIN) + 2 * N, N), 1)
                    packed = jnp.where(lane == base + t, low, packed)
                    packed = jnp.where(lane == base + WIN + t, high, packed)
                for kind, row in ((2, oy - 1), (3, oy + WIN)):
                    line = full[pl.ds(row, CZ, stride=FULL), :]
                    line = pltpu.roll(line, lax.rem(base + kind * WIN - ox + 2 * N, N), 1)
                    inside = jnp.logical_and(lane >= base + kind * WIN, lane < base + (kind + 1) * WIN)
                    packed = jnp.where(inside, line, packed)
            dst[...] = packed
        w_copy(s).start()

    extract(0, 0, 0)
    for i in range(PAIRS):
        even, odd = raw_rho[2 * i], raw_rho[2 * i + 1]
        rho_c[0, i + 1] = jnp.where(plane_parity == 0, even, odd)
        rho_c[1, i + 1] = jnp.where(plane_parity == 0, odd, even)

    pltpu.make_async_copy(raw_pot, raw_pot, in_sem.at[2]).wait()
    pltpu.make_async_copy(raw_src, raw_src, in_sem.at[3]).wait()
    for slot in range(SLOTS):
        def split(j, carry, slot=slot):
            for raw, scale, put in ((raw_pot, 4.0, 0), (raw_src, 0.25, 1)):
                even = scale * raw[slot, j, pl.ds(0, HALF, stride=2), :]
                odd = scale * raw[slot, j, pl.ds(1, HALF, stride=2), :]
                zero = jnp.where(fine_parity == 0, even, odd)
                one = jnp.where(fine_parity == 0, odd, even)
                if put == 0:
                    pa[slot, 0, j + 1, pl.ds(TOP, HALF), :] = zero
                    pa[slot, 1, j + 1, pl.ds(TOP, HALF), :] = one
                else:
                    src_c[slot, 0, j] = zero
                    src_c[slot, 1, j] = one
            return carry

        lax.fori_loop(0, HALF, split, 0)
        ox = anchors[0, p * SLOTS + slot]
        row, lane = iota((N, N), 0), lane_c
        sx[slot] = (row == ox + (lane % FINE) // 4).astype(jnp.float32).astype(jnp.bfloat16)
        wanted = slot * FINE + jnp.where(lane < FINE, 3 * WIN, 2 * WIN) + (lane % FINE) // 4
        ey[slot] = (row == wanted).astype(jnp.float32).astype(jnp.bfloat16)

    def coarse_pairs(b, role_c, role_b, role_out, q, pairs, first_half):
        cur, nxt = bufs[b], bufs[1 - b]
        other = cur if first_half else nxt
        outs = []
        for i in pairs:
            center = cur[role_c, i, rows, :]
            near = other[role_b, i, rows, :]
            below = other[role_b, max(i - 1, 0), rows, :]
            above = other[role_b, min(i + 1, PAIRS + 1), rows, :]
            outs.append(
                relaxed(
                    center,
                    (
                        near,
                        jnp.where(plane_parity == q, below, above),
                        other[role_b, i, pl.ds(TOP - 1, N), :],
                        other[role_b, i, pl.ds(TOP + 1, N), :],
                        jnp.where(lane_c == 0, 0.0, pltpu.roll(near, 1, 1)),
                        jnp.where(lane_c == N - 1, 0.0, pltpu.roll(near, N - 1, 1)),
                    ),
                    rho_c[q, i],
                )
            )
        for i, out in zip(pairs, outs):
            nxt[role_out, i, rows, :] = out

    def patch_half(slot, center_ref, role_c, other_ref, role_b, out_ref, role_out, q):
        data = pl.ds(TOP, HALF)

        def step(k, carry):
            j0 = k * JB
            b = [other_ref[slot, role_b, j0 + t, data, :] for t in range(JB + 2)]
            across = [pltpu.roll(jnp.where(y_first, b[t + 1], b[t]), FINE, 1) for t in range(JB + 1)]
            outs = []
            for t in range(JB):
                below = other_ref[slot, role_b, j0 + t + 1, pl.ds(TOP - 1, HALF), :]
                above = other_ref[slot, role_b, j0 + t + 1, pl.ds(TOP + 1, HALF), :]
                face = x_face[k * (JB // 2) + t // 2]
                near = b[t + 1]
                outs.append(
                    relaxed(
                        center_ref[slot, role_c, j0 + t + 1, data, :],
                        (
                            near,
                            jnp.where(fine_parity == q, below, above),
                            across[t],
                            across[t + 1],
                            jnp.where(x_first, face, pltpu.roll(near, 1, 1)),
                            jnp.where(x_last, face, pltpu.roll(near, N - 1, 1)),
                        ),
                        src_c[slot, q, j0 + t],
                    )
                )
            for t in range(JB):
                out_ref[slot, role_out, j0 + t + 1, data, :] = outs[t]
            return carry

        lax.fori_loop(0, HALF // JB, step, 0)

    def faces_of(slot, prev, nxt):
        data = pl.ds(TOP, HALF)
        w = 4.0 * w_rows[...]
        for t in range(WIN):
            low = jnp.broadcast_to(w[:, slot * FINE + t : slot * FINE + t + 1], (HALF, N))
            high = jnp.broadcast_to(w[:, slot * FINE + WIN + t : slot * FINE + WIN + t + 1], (HALF, N))
            x_face[t] = jnp.where(x_last, high, low)
        y_face = split_dot(w, ey[slot])
        oy = jnp.maximum(anchors[1, p * SLOTS + slot], 1)
        z_rows = jnp.concatenate([zplanes[0, pl.ds(oy, WIN), :], zplanes[1, pl.ds(oy, WIN), :]], axis=0)
        z_face = split_dot(4.0 * z_rows, sx[slot])
        for ref, role in ((prev, 0), (prev, 1), (nxt, 0)):
            ref[slot, role, 0, data, :] = y_face
            ref[slot, role, HALF + 1, data, :] = y_face
            for j in range(HALF):
                ref[slot, role, j + 1, TOP - 1 : TOP, :] = z_face[j // 2 : j // 2 + 1]
                ref[slot, role, j + 1, TOP + HALF : TOP + HALF + 1, :] = z_face[WIN + j // 2 : WIN + j // 2 + 1]

    patch_bufs = (pa, pb)

    def sweep(s, b, last):
        q = order[s]
        before = order[jnp.maximum(s - 1, 0)]
        first = jnp.where(s == 0, q, jnp.where(q == before, 0, 1))
        role0_colour = jnp.where(s == 0, 0, before)
        cur, nxt = bufs[b], bufs[1 - b]

        for side, ok, i in ((0, has_dn, 0), (1, has_up, PAIRS + 1)):
            @pl.when(ok)
            def _(side=side, i=i):
                for role in range(2):
                    halo_copy(s, b, role, 1 - side).wait_recv()
                    cur[role, i, rows, :] = halo_rx[s, role, side]

                @pl.when(s == 0)
                def _():
                    rho_copy(1 - side).wait_recv()
                    plane = rho_rx[side]
                    rho_c[0, i] = plane
                    rho_c[1, i] = plane

            @pl.when(jnp.logical_not(ok))
            def _(side=side, i=i):
                for role in range(2):
                    cur[role, i, rows, :] = jnp.zeros((N, N), jnp.float32)
                    rho_c[role, i] = jnp.zeros((N, N), jnp.float32)

        near_first, near_second = cur[0, p * (PAIRS + 1), rows, :], cur[1, p * (PAIRS + 1), rows, :]
        zplanes[p] = jnp.where(plane_parity == (role0_colour + 1 - p) % 2, near_first, near_second)

        def settle():
            for side, ok in ((0, has_dn), (1, has_up)):
                @pl.when(ok)
                def _(side=side):
                    for role in range(2):
                        halo_copy(s, b, role, side).wait_send()

                    @pl.when(s == 0)
                    def _():
                        rho_copy(side).wait_send()

            @pl.when(far_to_ok)
            def _():
                far_copy(s).wait_send()

            w_copy(s).wait_send()

        def send_next(role):
            if not last:
                send_halo(s + 1, 1 - b, role)
            else:
                @pl.when(s < SWEEPS - 1)
                def _():
                    send_halo(s + 1, 1 - b, role)

        coarse_pairs(b, first, 1 - first, 0, q, (1, PAIRS), True)
        send_next(0)
        coarse_pairs(b, first, 1 - first, 0, q, (0, 2), True)
        coarse_pairs(b, first, 1 - first, 0, q, (PAIRS - 1, PAIRS + 1), True)
        for ok, i in ((has_dn, 0), (has_up, PAIRS + 1)):
            @pl.when(jnp.logical_not(ok))
            def _(i=i):
                nxt[0, i, rows, :] = jnp.zeros((N, N), jnp.float32)
        coarse_pairs(b, 1 - first, 0, 1, 1 - q, (1, PAIRS), False)
        send_next(1)
        coarse_pairs(b, 1 - first, 0, 1, 1 - q, (2, PAIRS - 1), False)

        w_copy(s).wait_recv()
        mine, theirs = w_own[...], w_rx[s]
        lower = jnp.where(p == 0, mine, theirs)
        upper = jnp.where(p == 0, theirs, mine)
        for t in range(2):
            w_rows[pl.ds(t, CZ, stride=2), :] = lower
            w_rows[pl.ds(2 * CZ + t, CZ, stride=2), :] = upper

        @pl.when(far_from_ok)
        def _():
            far_copy(s).wait_recv()
            zplanes[1 - p] = far_rx[s]

        @pl.when(jnp.logical_not(far_from_ok))
        def _():
            zplanes[1 - p] = jnp.zeros((N, N), jnp.float32)

        settle()
        if not last:
            extract(s + 1, 1 - b, q)
        else:
            @pl.when(s < SWEEPS - 1)
            def _():
                extract(s + 1, 1 - b, q)

            @pl.when(s == SWEEPS - 1)
            def _():
                for i in range(PAIRS):
                    one, two = nxt[0, i + 1, rows, :], nxt[1, i + 1, rows, :]
                    raw_phi[2 * i] = jnp.where(plane_parity == q, one, two)
                    raw_phi[2 * i + 1] = jnp.where(plane_parity == q, two, one)
                pltpu.make_async_copy(raw_phi, coarse_hbm, out_sem.at[SLOTS]).start()

        for slot in range(SLOTS):
            now, new = patch_bufs[b], patch_bufs[1 - b]
            faces_of(slot, now, new)
            patch_half(slot, now, first, now, 1 - first, new, 0, q)
            patch_half(slot, now, 1 - first, new, 0, new, 1, 1 - q)
            if last:
                @pl.when(s == SWEEPS - 1)
                def _(slot=slot, new=new):
                    live = slot < owned[p]

                    def join(j, carry):
                        one = 0.25 * new[slot, 0, j + 1, pl.ds(TOP, HALF), :]
                        two = 0.25 * new[slot, 1, j + 1, pl.ds(TOP, HALF), :]
                        for odd in range(2):
                            z = pl.ds(odd, HALF, stride=2)
                            swept = jnp.where(fine_parity == (q + odd) % 2, one, two)
                            out_stage[slot, j, z, :] = jnp.where(live, swept, raw_pot[slot, j, z, :])
                        pltpu.make_async_copy(
                            out_stage.at[slot, j], patch_hbm.at[slot, :, columns(j)], out_sem.at[slot]
                        ).start()
                        return carry

                    lax.fori_loop(0, HALF, join, 0)

    def two_sweeps(t, carry):
        sweep(2 * t, 0, False)
        sweep(2 * t + 1, 1, True)
        return carry

    lax.fori_loop(0, SWEEPS // 2, two_sweeps, 0)
    pltpu.make_async_copy(raw_phi, coarse_hbm, out_sem.at[SLOTS]).wait()
    for slot in range(SLOTS):
        pltpu.make_async_copy(out_stage.at[slot], out_stage.at[slot], out_sem.at[slot]).wait()


def on_device(groups, phi, rho, pot, src, anchors, owned, order):
    f32, bf16 = jnp.float32, jnp.bfloat16
    dma = pltpu.SemaphoreType.DMA
    smem = pl.BlockSpec(memory_space=pltpu.SMEM)
    hbm = pl.BlockSpec(memory_space=pl.ANY)
    return pl.pallas_call(
        functools.partial(kernel, groups),
        out_shape=(jax.ShapeDtypeStruct(phi.shape, f32), jax.ShapeDtypeStruct(pot.shape, f32)),
        in_specs=[smem] * 3 + [hbm] * 4,
        out_specs=(hbm, hbm),
        scratch_shapes=[
            pltpu.VMEM((CZ, N, N), f32),
            pltpu.VMEM((CZ, N, N), f32),
            pltpu.VMEM((SLOTS, HALF, FINE, N), f32),
            pltpu.VMEM((SLOTS, HALF, FINE, N), f32),
            pltpu.VMEM((2, PAIRS + 2, N + 2 * TOP, N), f32),
            pltpu.VMEM((2, PAIRS + 2, N + 2 * TOP, N), f32),
            pltpu.VMEM((2, PAIRS + 2, N, N), f32),
            pltpu.VMEM((SWEEPS, 2, 2, N, N), f32),
            pltpu.VMEM((2, N, N), f32),
            pltpu.VMEM((CZ * FULL, N), f32),
            pltpu.VMEM((CZ, N), f32),
            pltpu.VMEM((CZ, N), f32),
            pltpu.VMEM((SWEEPS, CZ, N), f32),
            pltpu.VMEM((SWEEPS, N, N), f32),
            pltpu.VMEM((2, N, N), f32),
            pltpu.VMEM((HALF, N), f32),
            pltpu.VMEM((SLOTS, 2, HALF + 2, HALF + 2 * TOP, N), f32),
            pltpu.VMEM((SLOTS, 2, HALF + 2, HALF + 2 * TOP, N), f32),
            pltpu.VMEM((SLOTS, 2, HALF, HALF, N), f32),
            pltpu.VMEM((WIN, HALF, N), f32),
            pltpu.VMEM((SLOTS, N, N), bf16),
            pltpu.VMEM((SLOTS, N, N), bf16),
            pltpu.VMEM((SLOTS, HALF, FINE, N), f32),
            dma((4,)),
            dma((SLOTS + 1,)),
            dma((SWEEPS, 2, 2)),
            dma((SWEEPS, 2, 2)),
            dma((2,)),
            dma((2,)),
            dma,
            dma((SWEEPS,)),
            dma,
            dma((SWEEPS,)),
        ],
        compiler_params=pltpu.CompilerParams(
            collective_id=0, has_side_effects=True, vmem_limit_bytes=62 << 20
        ),
        name="smooth",
    )(anchors.T, owned, order, phi, rho, pot, src)


def solution(mesh):
    in_specs = (
        P(("slab", "patch"), None, None),
        P(("slab", "patch"), None, None),
        P(("slab", "patch"), None, None),
        P(("slab", "patch"), None, None),
        P("slab", None),
        P("slab"),
        P(),
    )
    out_specs = (P(("slab", "patch"), None, None), P(("slab", "patch"), None, None))
    return jax.shard_map(
        functools.partial(on_device, mesh.shape["slab"]),
        mesh=mesh, in_specs=in_specs, out_specs=out_specs, check_vma=False,
    )
```

time: 927 us -> 55.5 us (0.06)
  the two profiles are of different devices: /device:TPU:7 before, /device:TPU:6 now
where the time goes in v1:
time: 55.5 us; the launch traced here: 54.5 us
  Pallas kernels  48.9 us (88%)
  local copies, waits for them, and re-layouts  4.98 us (9%)
  between operations  0.64 us (1%)
    pallas_call x1, Pallas kernels, on_device(): pl.pallas_call(functools.partial(kernel, groups), out_shape=(jax.ShapeDty...  48.9 us
    unnamed x2, local copies, waits for them, and re-layouts  4.98 us

profile of v1, /device:TPU:6, one launch (start us, length us, event | category | flops | bytes accessed | tf_op | source)
XLA Modules:
  0.0 54.5 jit_solution(8454231404286870425)
XLA Ops:
  0.6 48.9 %smooth.1 = (f32[8,128,128]{2,1,0:T(8,128)}, f32[2,64,4096]{2,1,0:T(8,128)}) custom-call(s32[2,4]{1,0:T(2,128)} %bitcast.1, s32[2]{0:T(128)} %owned.1, s32[4]{0:T(128)} %order.1, f32[8,128,128]{2,1,0:T(8,128)} %phi_hbm.1, f32[8,128,128]{2,1,0:T(8,128)} %rho_hbm.1, f32[2,64,4096]{2,1,0:T(8,128)} %pot_hbm.1, f32[2,64,4096]{2,1,0:T(8,128)} %src_hbm.1), custom_call_target="tpu_custom_call" | custom-call | tf_op jit(solution)/shard_map/smooth/pallas_call | solution.py:450
  49.5 1.9 %copy.11 = f32[8,128,128]{2,1,0:T(8,128)} copy(f32[8,128,128]{2,1,0:T(8,128)} %get-tuple-element.4) | data formatting | bytes 1048576
  51.4 3.1 %copy.12 = f32[2,64,4096]{2,1,0:T(8,128)} copy(f32[2,64,4096]{2,1,0:T(8,128)} %get-tuple-element.5) | data formatting | bytes 4194304

commit v2 on v1

v2 whole, which is shorter than its diff:
```python
import functools

import jax
import jax.numpy as jnp
from jax import lax
from jax.experimental import pallas as pl
from jax.experimental.pallas import tpu as pltpu
from jax.sharding import PartitionSpec as P

MESH = pl.DeviceIdType.MESH
SWEEPS = 4
N = 128
CZ = 8
PAIRS = CZ // 2
SLOTS = 2
FINE = 64
HALF = FINE // 2
WIN = 16
TOP = 8
FULL = N + 8
JB = 8


def relaxed(center, neighbours, source):
    r_sum = rv_sum = v_sum = None
    for value in neighbours:
        r = pl.reciprocal(1.0 + jnp.abs(value - center), approx=True)
        rv = r * value
        r_sum = r if r_sum is None else r_sum + r
        rv_sum = rv if rv_sum is None else rv_sum + rv
        v_sum = value if v_sum is None else v_sum + value
    return (rv_sum + (v_sum - source)) * pl.reciprocal(6.0 + r_sum, approx=True)


def iota(shape, dim):
    return lax.broadcasted_iota(jnp.int32, shape, dim)


def split_dot(rows, onehot):
    high = rows.astype(jnp.bfloat16)
    low = (rows - high.astype(jnp.float32)).astype(jnp.bfloat16)
    return jnp.dot(high, onehot, preferred_element_type=jnp.float32) + jnp.dot(
        low, onehot, preferred_element_type=jnp.float32
    )


def kernel(
    groups,
    anchors, owned, order, phi_hbm, rho_hbm, pot_hbm, src_hbm,
    coarse_hbm, patch_hbm,
    full, raw_rho, raw_pot, raw_src,
    ca, cb, halo, rho_c, rho_h, near_rx, half_send, half_rx, rho_send, rho_rx,
    w_own, w_send, w_rx, far_rx, zplanes, w_rows, pa, pb, src_c, x_face, sx, ey, coarse_stage, out_stage,
    in_sem, out_sem, near_ssem, near_rsem, half_ssem, half_rsem, rho_ssem, rho_rsem,
    w_ssem, w_rsem, far_ssem, far_rsem,
):
    g = lax.axis_index("slab")
    p = lax.axis_index("patch")
    has_up = jnp.logical_or(g < groups - 1, p == 0)
    has_dn = jnp.logical_or(g > 0, p == 1)
    far_to_ok = jnp.where(p == 0, g > 0, g < groups - 1)
    far_from_ok = jnp.where(p == 0, g < groups - 1, g > 0)
    wrap = lambda v: lax.rem(v + groups, groups)
    up = (wrap(g + p), 1 - p)
    dn = (wrap(g - 1 + p), 1 - p)
    partner = (g, 1 - p)
    far_to = (wrap(g + 2 * p - 1), p)
    far_from = (wrap(g + 1 - 2 * p), p)
    sides = ((0, has_dn), (1, has_up))

    barrier = pltpu.get_barrier_semaphore()
    greeted = ((up, has_up), (dn, has_dn), (far_to, far_to_ok), (far_from, far_from_ok))
    for device, ok in greeted:
        @pl.when(ok)
        def _(device=device):
            pl.semaphore_signal(barrier, inc=1, device_id=device, device_id_type=MESH)

    def plane(z):
        return pl.ds(z * FULL, N)

    loads = [pltpu.make_async_copy(phi_hbm.at[z], full.at[plane(z)], in_sem.at[z]) for z in range(CZ)]
    loads.append(pltpu.make_async_copy(rho_hbm, raw_rho, in_sem.at[CZ]))
    for load in loads:
        load.start()

    def columns(j):
        return pl.ds(pl.multiple_of(j * N, N), N)

    def fetch(j, carry):
        for slot in range(SLOTS):
            pltpu.make_async_copy(
                pot_hbm.at[slot, :, columns(j)], raw_pot.at[slot, j], in_sem.at[CZ + 1]
            ).start()
            pltpu.make_async_copy(
                src_hbm.at[slot, :, columns(j)], raw_src.at[slot, j], in_sem.at[CZ + 2]
            ).start()
        return carry

    rows = pl.ds(TOP, N)
    bufs = (ca, cb)

    def near_copy(s, side):
        return pltpu.make_async_remote_copy(
            src_ref=full.at[plane(side * (CZ - 1))], dst_ref=near_rx.at[s, 1 - side],
            send_sem=near_ssem.at[side], recv_sem=near_rsem.at[s, 1 - side],
            device_id=(dn, up)[side], device_id_type=MESH,
        )

    def half_copy(s, side):
        return pltpu.make_async_remote_copy(
            src_ref=half_send.at[side], dst_ref=half_rx.at[s, 1 - side],
            send_sem=half_ssem.at[side], recv_sem=half_rsem.at[s, 1 - side],
            device_id=(dn, up)[side], device_id_type=MESH,
        )

    def rho_copy(which, side):
        return pltpu.make_async_remote_copy(
            src_ref=rho_send.at[which, side], dst_ref=rho_rx.at[which, 1 - side],
            send_sem=rho_ssem.at[which, side], recv_sem=rho_rsem.at[which, 1 - side],
            device_id=(dn, up)[side], device_id_type=MESH,
        )

    def w_copy(s):
        return pltpu.make_async_remote_copy(
            src_ref=w_send, dst_ref=w_rx.at[s], send_sem=w_ssem, recv_sem=w_rsem.at[s],
            device_id=partner, device_id_type=MESH,
        )

    def far_copy(s):
        return pltpu.make_async_remote_copy(
            src_ref=full.at[pl.ds(p * ((CZ - 1) * FULL), N)], dst_ref=far_rx.at[s],
            send_sem=far_ssem, recv_sem=far_rsem.at[s],
            device_id=far_to, device_id_type=MESH,
        )

    plane_parity = (iota((N, N), 0) + iota((N, N), 1)) % 2
    half_parity = (iota((FINE, N), 0) + iota((FINE, N), 1)) % 2
    lane_c = iota((N, N), 1)
    lane_p = iota((HALF, N), 1)
    fine_parity = (lane_p // FINE + lane_p) % 2
    x_first = lane_p % FINE == 0
    x_last = lane_p % FINE == FINE - 1
    y_first = lane_p < FINE

    def folded(cells, parity):
        return jnp.where(half_parity == parity, cells[:FINE], pltpu.roll(cells[FINE:], 1, 1))

    def unfolded(cells):
        return jnp.concatenate([cells, pltpu.roll(cells, N - 1, 1)], axis=0)

    for ref, lead in ((ca, 2), (cb, 2), (halo, 0)):
        for role in range(max(lead, 1)):
            for i in range(PAIRS + 2 if lead else 2):
                where = (role, i) if lead else (i,)
                ref[(*where, slice(0, TOP), slice(None))] = jnp.zeros((TOP, N), jnp.float32)
                ref[(*where, slice(TOP + N, None), slice(None))] = jnp.zeros((TOP, N), jnp.float32)

    def pack_faces():
        lane = iota((CZ, N), 1)
        for whose, dst in ((1 - p, w_send), (p, w_own)):
            packed = jnp.zeros((CZ, N), jnp.float32)
            for k in range(SLOTS):
                ox = anchors[0, whose * SLOTS + k]
                oy = jnp.maximum(anchors[1, whose * SLOTS + k], 1)
                base = k * FINE
                for t in range(WIN):
                    line = full[pl.ds(oy + t, CZ, stride=FULL), :]
                    low = pltpu.roll(line, lax.rem(base + t - (ox - 1) + 2 * N, N), 1)
                    high = pltpu.roll(line, lax.rem(base + WIN + t - (ox + WIN) + 2 * N, N), 1)
                    packed = jnp.where(lane == base + t, low, packed)
                    packed = jnp.where(lane == base + WIN + t, high, packed)
                for kind, row in ((2, oy - 1), (3, oy + WIN)):
                    line = full[pl.ds(row, CZ, stride=FULL), :]
                    line = pltpu.roll(line, lax.rem(base + kind * WIN - ox + 2 * N, N), 1)
                    inside = jnp.logical_and(lane >= base + kind * WIN, lane < base + (kind + 1) * WIN)
                    packed = jnp.where(inside, line, packed)
            dst[...] = packed

    q_start = order[0]
    for z in range(CZ):
        loads[z].wait()
    for i in range(PAIRS):
        even, odd = full[plane(2 * i), :], full[plane(2 * i + 1), :]
        ca[0, i + 1, rows, :] = jnp.where(plane_parity == 0, even, odd)
        ca[1, i + 1, rows, :] = jnp.where(plane_parity == 0, odd, even)
    half_send[0] = folded(full[plane(1), :], q_start)
    half_send[1] = folded(full[plane(CZ - 2), :], 1 - q_start)
    loads[CZ].wait()
    for which in range(2):
        rho_send[which, 0] = folded(raw_rho[0], (q_start + which) % 2)
        rho_send[which, 1] = folded(raw_rho[CZ - 1], (q_start + which + 1) % 2)
    pack_faces()

    pl.semaphore_wait(barrier, sum(ok.astype(jnp.int32) for _, ok in greeted))

    def start_halo(s):
        for make in (near_copy, half_copy):
            for side, ok in sides:
                @pl.when(ok)
                def _(make=make, side=side):
                    make(s, side).start()

    def start_rho(which):
        for side, ok in sides:
            @pl.when(ok)
            def _(side=side):
                rho_copy(which, side).start()

    def start_far(s):
        @pl.when(far_to_ok)
        def _():
            far_copy(s).start()

    start_halo(0)
    start_rho(0)
    start_far(0)
    w_copy(0).start()
    start_rho(1)
    lax.fori_loop(0, HALF, fetch, 0)

    for i in range(PAIRS):
        even, odd = raw_rho[2 * i], raw_rho[2 * i + 1]
        rho_c[0, i] = jnp.where(plane_parity == 0, even, odd)
        rho_c[1, i] = jnp.where(plane_parity == 0, odd, even)

    for slot in range(SLOTS):
        ox = anchors[0, p * SLOTS + slot]
        row, lane = iota((N, N), 0), lane_c
        sx[slot] = (row == ox + (lane % FINE) // 4).astype(jnp.float32).astype(jnp.bfloat16)
        wanted = slot * FINE + jnp.where(lane < FINE, 3 * WIN, 2 * WIN) + (lane % FINE) // 4
        ey[slot] = (row == wanted).astype(jnp.float32).astype(jnp.bfloat16)
    pltpu.make_async_copy(raw_pot, raw_pot, in_sem.at[CZ + 1]).wait()
    pltpu.make_async_copy(raw_src, raw_src, in_sem.at[CZ + 2]).wait()

    def split(j, carry):
        for slot in range(SLOTS):
            for raw, scale, put in ((raw_pot, 4.0, 0), (raw_src, 0.25, 1)):
                even = scale * raw[slot, j, pl.ds(0, HALF, stride=2), :]
                odd = scale * raw[slot, j, pl.ds(1, HALF, stride=2), :]
                zero = jnp.where(fine_parity == 0, even, odd)
                one = jnp.where(fine_parity == 0, odd, even)
                if put == 0:
                    pa[slot, 0, j + 1, pl.ds(TOP, HALF), :] = zero
                    pa[slot, 1, j + 1, pl.ds(TOP, HALF), :] = one
                else:
                    src_c[slot, 0, j] = zero
                    src_c[slot, 1, j] = one
        return carry

    lax.fori_loop(0, HALF, split, 0)

    def coarse_pairs(s, b, first, q, pairs, first_half):
        cur, nxt = bufs[b], bufs[1 - b]
        which = jnp.where(q == q_start, 0, 1)

        def cell(i):
            if i in (0, PAIRS + 1):
                return near_rx[s, i // PAIRS]
            return cur[first if first_half else 1 - first, i, rows, :]

        def other(i, at):
            if not first_half:
                return nxt[0, i, at, :]
            if i in (0, PAIRS + 1):
                return halo[i // PAIRS, at, :]
            return cur[1 - first, i, at, :]

        outs = []
        for i in pairs:
            near = other(i, rows)
            if i == 0:
                second = other(1, rows)
            elif i == PAIRS + 1:
                second = other(PAIRS, rows)
            else:
                second = jnp.where(plane_parity == q, other(i - 1, rows), other(i + 1, rows))
            source = rho_h[which, i // PAIRS] if i in (0, PAIRS + 1) else rho_c[q, i - 1]
            outs.append(
                relaxed(
                    cell(i),
                    (
                        near,
                        second,
                        other(i, pl.ds(TOP - 1, N)),
                        other(i, pl.ds(TOP + 1, N)),
                        jnp.where(lane_c == 0, 0.0, pltpu.roll(near, 1, 1)),
                        jnp.where(lane_c == N - 1, 0.0, pltpu.roll(near, N - 1, 1)),
                    ),
                    source,
                )
            )
        for i, out in zip(pairs, outs):
            nxt[0 if first_half else 1, i, rows, :] = out

    def patch_half(slot, center_ref, role_c, other_ref, role_b, out_ref, role_out, q):
        data = pl.ds(TOP, HALF)

        def step(k, carry):
            j0 = k * JB
            b = [other_ref[slot, role_b, j0 + t, data, :] for t in range(JB + 2)]
            across = [pltpu.roll(jnp.where(y_first, b[t + 1], b[t]), FINE, 1) for t in range(JB + 1)]
            outs = []
            for t in range(JB):
                below = other_ref[slot, role_b, j0 + t + 1, pl.ds(TOP - 1, HALF), :]
                above = other_ref[slot, role_b, j0 + t + 1, pl.ds(TOP + 1, HALF), :]
                face = x_face[k * (JB // 2) + t // 2]
                near = b[t + 1]
                outs.append(
                    relaxed(
                        center_ref[slot, role_c, j0 + t + 1, data, :],
                        (
                            near,
                            jnp.where(fine_parity == q, below, above),
                            across[t],
                            across[t + 1],
                            jnp.where(x_first, face, pltpu.roll(near, 1, 1)),
                            jnp.where(x_last, face, pltpu.roll(near, N - 1, 1)),
                        ),
                        src_c[slot, q, j0 + t],
                    )
                )
            for t in range(JB):
                out_ref[slot, role_out, j0 + t + 1, data, :] = outs[t]
            return carry

        lax.fori_loop(0, HALF // JB, step, 0)

    def faces_of(s, slot, prev, nxt):
        data = pl.ds(TOP, HALF)
        w = 4.0 * w_rows[...]
        for t in range(WIN):
            low = jnp.broadcast_to(w[:, slot * FINE + t : slot * FINE + t + 1], (HALF, N))
            high = jnp.broadcast_to(w[:, slot * FINE + WIN + t : slot * FINE + WIN + t + 1], (HALF, N))
            x_face[t] = jnp.where(x_last, high, low)
        y_face = split_dot(w, ey[slot])
        oy = jnp.maximum(anchors[1, p * SLOTS + slot], 1)
        z_rows = jnp.concatenate([zplanes[0, pl.ds(oy, WIN), :], zplanes[1, pl.ds(oy, WIN), :]], axis=0)
        z_face = split_dot(z_rows, sx[slot])
        for ref, role in ((prev, 0), (prev, 1), (nxt, 0)):
            ref[slot, role, 0, data, :] = y_face
            ref[slot, role, HALF + 1, data, :] = y_face
            for j in range(HALF):
                ref[slot, role, j + 1, TOP - 1 : TOP, :] = z_face[j // 2 : j // 2 + 1]
                ref[slot, role, j + 1, TOP + HALF : TOP + HALF + 1, :] = z_face[WIN + j // 2 : WIN + j // 2 + 1]

    patch_bufs = (pa, pb)

    def sweep(s, b, may_end):
        q = order[s]
        before = order[jnp.maximum(s - 1, 0)]
        first = jnp.where(s == 0, q, jnp.where(q == before, 0, 1))
        cur, nxt = bufs[b], bufs[1 - b]

        def unless_last(do):
            if may_end:
                pl.when(s < SWEEPS - 1)(do)
            else:
                do()

        coarse_pairs(s, b, first, q, (2, PAIRS - 1), True)
        for side, ok in sides:
            @pl.when(ok)
            def _(side=side):
                near_copy(s, 1 - side).wait_recv()
                half_copy(s, 1 - side).wait_recv()
                second = unfolded(half_rx[s, side])
                halo[side, rows, :] = jnp.where(
                    plane_parity == (1 - q if side == 0 else q), second, near_rx[s, side]
                )

                @pl.when(s == b)
                def _():
                    rho_copy(b, 1 - side).wait_recv()
                    rho_h[b, side] = unfolded(rho_rx[b, side])

            @pl.when(jnp.logical_not(ok))
            def _(side=side):
                halo[side, rows, :] = jnp.zeros((N, N), jnp.float32)

        coarse_pairs(s, b, first, q, (1, PAIRS), True)
        coarse_pairs(s, b, first, q, (0, PAIRS + 1), True)
        for side, ok in sides:
            @pl.when(jnp.logical_not(ok))
            def _(side=side):
                nxt[0, side * (PAIRS + 1), rows, :] = jnp.zeros((N, N), jnp.float32)
        coarse_pairs(s, b, first, 1 - q, (1, PAIRS), False)

        for side, ok in sides:
            @pl.when(ok)
            def _(side=side):
                near_copy(s, side).wait_send()
                half_copy(s, side).wait_send()

                @pl.when(s == b)
                def _():
                    rho_copy(b, side).wait_send()

        @pl.when(far_to_ok)
        def _():
            far_copy(s).wait_send()

        w_copy(s).wait_send()

        def whole(z):
            role = z % 2
            i = z // 2 + 1
            return jnp.where(plane_parity == q, nxt[role, i, rows, :], nxt[1 - role, i, rows, :])

        def send_outer():
            full[plane(0), :] = whole(0)
            full[plane(CZ - 1), :] = whole(CZ - 1)
            q_next = order[jnp.minimum(s + 1, SWEEPS - 1)]
            read = jnp.where(q_next == q, 1, 0)
            half_send[0] = folded(nxt[read, 1, rows, :], q_next)
            half_send[1] = folded(nxt[read, PAIRS, rows, :], 1 - q_next)
            start_halo(s + 1)
            start_far(s + 1)

        unless_last(send_outer)
        coarse_pairs(s, b, first, 1 - q, (2, PAIRS - 1), False)

        w_copy(s).wait_recv()
        mine, theirs = w_own[...], w_rx[s]
        lower = jnp.where(p == 0, mine, theirs)
        upper = jnp.where(p == 0, theirs, mine)
        for t in range(2):
            w_rows[pl.ds(t, CZ, stride=2), :] = lower
            w_rows[pl.ds(2 * CZ + t, CZ, stride=2), :] = upper

        def send_faces():
            for z in range(1, CZ - 1):
                full[plane(z), :] = whole(z)
            pack_faces()
            w_copy(s + 1).start()

        unless_last(send_faces)
        if may_end:
            @pl.when(s == SWEEPS - 1)
            def _():
                for z in range(CZ):
                    coarse_stage[z] = whole(z)
                pltpu.make_async_copy(coarse_stage, coarse_hbm, out_sem.at[SLOTS]).start()

        @pl.when(far_from_ok)
        def _():
            far_copy(s).wait_recv()

        near_ok = jnp.where(p == 0, has_dn, has_up)
        zplanes[p] = jnp.where(near_ok, 4.0 * near_rx[s, p], 0.0)
        zplanes[1 - p] = jnp.where(far_from_ok, 4.0 * far_rx[s], 0.0)
        for slot in range(SLOTS):
            now, new = patch_bufs[b], patch_bufs[1 - b]
            faces_of(s, slot, now, new)
            patch_half(slot, now, first, now, 1 - first, new, 0, q)
            patch_half(slot, now, 1 - first, new, 0, new, 1, 1 - q)
            if may_end:
                @pl.when(s == SWEEPS - 1)
                def _(slot=slot, new=new):
                    live = slot < owned[p]

                    def join(j, carry):
                        one = 0.25 * new[slot, 0, j + 1, pl.ds(TOP, HALF), :]
                        two = 0.25 * new[slot, 1, j + 1, pl.ds(TOP, HALF), :]
                        for odd in range(2):
                            z = pl.ds(odd, HALF, stride=2)
                            swept = jnp.where(fine_parity == (q + odd) % 2, one, two)
                            out_stage[slot, j, z, :] = jnp.where(live, swept, raw_pot[slot, j, z, :])
                        pltpu.make_async_copy(
                            out_stage.at[slot, j], patch_hbm.at[slot, :, columns(j)], out_sem.at[slot]
                        ).start()
                        return carry

                    lax.fori_loop(0, HALF, join, 0)

    def two_sweeps(t, carry):
        sweep(2 * t, 0, False)
        sweep(2 * t + 1, 1, True)
        return carry

    lax.fori_loop(0, SWEEPS // 2, two_sweeps, 0)
    pltpu.make_async_copy(coarse_stage, coarse_hbm, out_sem.at[SLOTS]).wait()
    for slot in range(SLOTS):
        pltpu.make_async_copy(out_stage.at[slot], out_stage.at[slot], out_sem.at[slot]).wait()


def on_device(groups, phi, rho, pot, src, anchors, owned, order):
    f32, bf16 = jnp.float32, jnp.bfloat16
    dma = pltpu.SemaphoreType.DMA
    smem = pl.BlockSpec(memory_space=pltpu.SMEM)
    hbm = pl.BlockSpec(memory_space=pltpu.HBM)
    anywhere = pl.BlockSpec(memory_space=pl.ANY)
    return pl.pallas_call(
        functools.partial(kernel, groups),
        out_shape=(pltpu.VMEM(phi.shape, f32), pltpu.VMEM(pot.shape, f32)),
        in_specs=[smem] * 3 + [hbm] * 4,
        out_specs=(anywhere, anywhere),
        scratch_shapes=[
            pltpu.VMEM((CZ * FULL, N), f32),
            pltpu.VMEM((CZ, N, N), f32),
            pltpu.VMEM((SLOTS, HALF, FINE, N), f32),
            pltpu.VMEM((SLOTS, HALF, FINE, N), f32),
            pltpu.VMEM((2, PAIRS + 2, N + 2 * TOP, N), f32),
            pltpu.VMEM((2, PAIRS + 2, N + 2 * TOP, N), f32),
            pltpu.VMEM((2, N + 2 * TOP, N), f32),
            pltpu.VMEM((2, PAIRS, N, N), f32),
            pltpu.VMEM((2, 2, N, N), f32),
            pltpu.VMEM((SWEEPS, 2, N, N), f32),
            pltpu.VMEM((2, FINE, N), f32),
            pltpu.VMEM((SWEEPS, 2, FINE, N), f32),
            pltpu.VMEM((2, 2, FINE, N), f32),
            pltpu.VMEM((2, 2, FINE, N), f32),
            pltpu.VMEM((CZ, N), f32),
            pltpu.VMEM((CZ, N), f32),
            pltpu.VMEM((SWEEPS, CZ, N), f32),
            pltpu.VMEM((SWEEPS, N, N), f32),
            pltpu.VMEM((2, N, N), f32),
            pltpu.VMEM((HALF, N), f32),
            pltpu.VMEM((SLOTS, 2, HALF + 2, HALF + 2 * TOP, N), f32),
            pltpu.VMEM((SLOTS, 2, HALF + 2, HALF + 2 * TOP, N), f32),
            pltpu.VMEM((SLOTS, 2, HALF, HALF, N), f32),
            pltpu.VMEM((WIN, HALF, N), f32),
            pltpu.VMEM((SLOTS, N, N), bf16),
            pltpu.VMEM((SLOTS, N, N), bf16),
            pltpu.VMEM((CZ, N, N), f32),
            pltpu.VMEM((SLOTS, HALF, FINE, N), f32),
            dma((CZ + 3,)),
            dma((SLOTS + 1,)),
            dma((2,)),
            dma((SWEEPS, 2)),
            dma((2,)),
            dma((SWEEPS, 2)),
            dma((2, 2)),
            dma((2, 2)),
            dma,
            dma((SWEEPS,)),
            dma,
            dma((SWEEPS,)),
        ],
        compiler_params=pltpu.CompilerParams(
            collective_id=0, has_side_effects=True, vmem_limit_bytes=54000000
        ),
        name="smooth",
    )(anchors.T, owned, order, phi, rho, pot, src)


def solution(mesh):
    in_specs = (
        P(("slab", "patch"), None, None),
        P(("slab", "patch"), None, None),
        P(("slab", "patch"), None, None),
        P(("slab", "patch"), None, None),
        P("slab", None),
        P("slab"),
        P(),
    )
    out_specs = (P(("slab", "patch"), None, None), P(("slab", "patch"), None, None))
    return jax.shard_map(
        functools.partial(on_device, mesh.shape["slab"]),
        mesh=mesh, in_specs=in_specs, out_specs=out_specs, check_vma=False,
    )
```

time: 55.5 us -> 48.6 us (0.88); the launches traced: 54.5 us -> 48.4 us
  Pallas kernels: 48.9 us -> 45.6 us
  local copies, waits for them, and re-layouts: 4.98 us -> 2.11 us
    pallas_call x1, Pallas kernels: 48.9 us -> 45.6 us  [on_device(): pl.pallas_call(functools.partial(kernel, groups), out_shape=(pltpu.VMEM(p...]
    unnamed x2, local copies, waits for them, and re-layouts: 4.98 us -> 2.11 us
where the time goes in v2:
time: 48.6 us; the launch traced here: 48.4 us
  Pallas kernels  45.6 us (94%)
  local copies, waits for them, and re-layouts  2.11 us (4%)
  between operations  0.64 us (1%)
    pallas_call x1, Pallas kernels, on_device(): pl.pallas_call(functools.partial(kernel, groups), out_shape=(pltpu.VMEM(p...  45.6 us
    unnamed x2, local copies, waits for them, and re-layouts  2.11 us

profile of v2, /device:TPU:6, one launch (start us, length us, event | category | flops | bytes accessed | tf_op | source)
XLA Modules:
  0.0 48.4 jit_solution(8553114520433993665)
XLA Ops:
  0.6 45.6 %smooth.1 = (f32[8,128,128]{2,1,0:T(8,128)S(1)}, f32[2,64,4096]{2,1,0:T(8,128)S(1)}) custom-call(s32[2,4]{1,0:T(2,128)} %bitcast.1, s32[2]{0:T(128)} %owned.1, s32[4]{0:T(128)} %order.1, f32[8,128,128]{2,1,0:T(8,128)} %phi_hbm.1, f32[8,128,128]{2,1,0:T(8,128)} %rho_hbm.1, f32[2,64,4096]{2,1,0:T(8,128)} %pot_hbm.1, f32[2,64,4096]{2,1,0:T(8,128)} %src_hbm.1), custom_call_target="tpu_custom_call" | custom-call | tf_op jit(solution)/shard_map/smooth/pallas_call | solution.py:492
  46.3 0.8 %copy.11 = f32[8,128,128]{2,1,0:T(8,128)} copy(f32[8,128,128]{2,1,0:T(8,128)S(1)} %get-tuple-element.2) | data formatting | bytes 1048576
  47.1 1.3 %copy.12 = f32[2,64,4096]{2,1,0:T(8,128)} copy(f32[2,64,4096]{2,1,0:T(8,128)S(1)} %get-tuple-element.3) | data formatting | bytes 4194304

commit v3 on v2

--- a/solution.py
+++ b/solution.py
@@ -18,6 +18,7 @@
 WIN = 16
 TOP = 8
 FULL = N + 8
+JOIN = 4
 JB = 8
 
 
@@ -49,9 +50,9 @@
     anchors, owned, order, phi_hbm, rho_hbm, pot_hbm, src_hbm,
     coarse_hbm, patch_hbm,
     full, raw_rho, raw_pot, raw_src,
-    ca, cb, halo, rho_c, rho_h, near_rx, half_send, half_rx, rho_send, rho_rx,
+    ca, cb, halo, rho_c, rho_h, near_rx, near, pair_send, pair_rx, rho_send, rho_rx,
     w_own, w_send, w_rx, far_rx, zplanes, w_rows, pa, pb, src_c, x_face, sx, ey, coarse_stage, out_stage,
-    in_sem, out_sem, near_ssem, near_rsem, half_ssem, half_rsem, rho_ssem, rho_rsem,
+    in_sem, out_sem, near_ssem, near_rsem, pair_ssem, pair_rsem, rho_ssem, rho_rsem,
     w_ssem, w_rsem, far_ssem, far_rsem,
 ):
     g = lax.axis_index("slab")
@@ -99,17 +100,17 @@
     rows = pl.ds(TOP, N)
     bufs = (ca, cb)
 
-    def near_copy(s, side):
+    def near_copy(side):
         return pltpu.make_async_remote_copy(
-            src_ref=full.at[plane(side * (CZ - 1))], dst_ref=near_rx.at[s, 1 - side],
-            send_sem=near_ssem.at[side], recv_sem=near_rsem.at[s, 1 - side],
+            src_ref=full.at[plane(side * (CZ - 1))], dst_ref=near_rx.at[1 - side],
+            send_sem=near_ssem.at[side], recv_sem=near_rsem.at[1 - side],
             device_id=(dn, up)[side], device_id_type=MESH,
         )
 
-    def half_copy(s, side):
+    def pair_copy(s, side, at):
         return pltpu.make_async_remote_copy(
-            src_ref=half_send.at[side], dst_ref=half_rx.at[s, 1 - side],
-            send_sem=half_ssem.at[side], recv_sem=half_rsem.at[s, 1 - side],
+            src_ref=pair_send.at[side, at], dst_ref=pair_rx.at[s, 1 - side, at],
+            send_sem=pair_ssem.at[side], recv_sem=pair_rsem.at[s, 1 - side],
             device_id=(dn, up)[side], device_id_type=MESH,
         )
 
@@ -183,8 +184,8 @@
         even, odd = full[plane(2 * i), :], full[plane(2 * i + 1), :]
         ca[0, i + 1, rows, :] = jnp.where(plane_parity == 0, even, odd)
         ca[1, i + 1, rows, :] = jnp.where(plane_parity == 0, odd, even)
-    half_send[0] = folded(full[plane(1), :], q_start)
-    half_send[1] = folded(full[plane(CZ - 2), :], 1 - q_start)
+    pair_send[0, FINE:, :] = folded(full[plane(1), :], q_start)
+    pair_send[1, FINE:, :] = folded(full[plane(CZ - 2), :], 1 - q_start)
     loads[CZ].wait()
     for which in range(2):
         rho_send[which, 0] = folded(raw_rho[0], (q_start + which) % 2)
@@ -193,13 +194,6 @@
 
     pl.semaphore_wait(barrier, sum(ok.astype(jnp.int32) for _, ok in greeted))
 
-    def start_halo(s):
-        for make in (near_copy, half_copy):
-            for side, ok in sides:
-                @pl.when(ok)
-                def _(make=make, side=side):
-                    make(s, side).start()
-
     def start_rho(which):
         for side, ok in sides:
             @pl.when(ok)
@@ -211,7 +205,15 @@
         def _():
             far_copy(s).start()
 
-    start_halo(0)
+    both, second_only = pl.ds(0, N), pl.ds(FINE, FINE)
+    for side, ok in sides:
+        @pl.when(ok)
+        def _(side=side):
+            near_copy(side).start()
+    for side, ok in sides:
+        @pl.when(ok)
+        def _(side=side):
+            pair_copy(0, side, second_only).start()
     start_rho(0)
     start_far(0)
     w_copy(0).start()
@@ -255,7 +257,7 @@
 
         def cell(i):
             if i in (0, PAIRS + 1):
-                return near_rx[s, i // PAIRS]
+                return near[i // PAIRS]
             return cur[first if first_half else 1 - first, i, rows, :]
 
         def other(i, at):
@@ -267,7 +269,7 @@
 
         outs = []
         for i in pairs:
-            near = other(i, rows)
+            here = other(i, rows)
             if i == 0:
                 second = other(1, rows)
             elif i == PAIRS + 1:
@@ -279,12 +281,12 @@
                 relaxed(
                     cell(i),
                     (
-                        near,
+                        here,
                         second,
                         other(i, pl.ds(TOP - 1, N)),
                         other(i, pl.ds(TOP + 1, N)),
-                        jnp.where(lane_c == 0, 0.0, pltpu.roll(near, 1, 1)),
-                        jnp.where(lane_c == N - 1, 0.0, pltpu.roll(near, N - 1, 1)),
+                        jnp.where(lane_c == 0, 0.0, pltpu.roll(here, 1, 1)),
+                        jnp.where(lane_c == N - 1, 0.0, pltpu.roll(here, N - 1, 1)),
                     ),
                     source,
                 )
@@ -361,11 +363,26 @@
         for side, ok in sides:
             @pl.when(ok)
             def _(side=side):
-                near_copy(s, 1 - side).wait_recv()
-                half_copy(s, 1 - side).wait_recv()
-                second = unfolded(half_rx[s, side])
+                def start_of_all():
+                    near_copy(1 - side).wait_recv()
+                    pair_copy(s, 1 - side, second_only).wait_recv()
+                    near[side] = near_rx[side]
+
+                def later():
+                    pair_copy(s, 1 - side, both).wait_recv()
+                    mine = plane_parity == (1 - before if side == 0 else before)
+                    near[side] = jnp.where(
+                        mine, cur[0, side * (PAIRS + 1), rows, :], unfolded(pair_rx[s, side, :FINE, :])
+                    )
+
+                if b == 0:
+                    pl.when(s == 0)(start_of_all)
+                    pl.when(s > 0)(later)
+                else:
+                    later()
+                second = unfolded(pair_rx[s, side, FINE:, :])
                 halo[side, rows, :] = jnp.where(
-                    plane_parity == (1 - q if side == 0 else q), second, near_rx[s, side]
+                    plane_parity == (1 - q if side == 0 else q), second, near[side]
                 )
 
                 @pl.when(s == b)
@@ -388,8 +405,17 @@
         for side, ok in sides:
             @pl.when(ok)
             def _(side=side):
-                near_copy(s, side).wait_send()
-                half_copy(s, side).wait_send()
+                if b == 0:
+                    @pl.when(s == 0)
+                    def _():
+                        near_copy(side).wait_send()
+                        pair_copy(s, side, second_only).wait_send()
+
+                    @pl.when(s > 0)
+                    def _():
+                        pair_copy(s, side, both).wait_send()
+                else:
+                    pair_copy(s, side, both).wait_send()
 
                 @pl.when(s == b)
                 def _():
@@ -407,13 +433,20 @@
             return jnp.where(plane_parity == q, nxt[role, i, rows, :], nxt[1 - role, i, rows, :])
 
         def send_outer():
+            q_next = order[jnp.minimum(s + 1, SWEEPS - 1)]
+            read = jnp.where(q_next == q, 1, 0)
+            for side, ok in sides:
+                i = PAIRS if side else 1
+                last, ahead = (q, 1 - q_next) if side else (1 - q, q_next)
+                pair_send[side, :FINE, :] = folded(nxt[1, i, rows, :], last)
+                pair_send[side, FINE:, :] = folded(nxt[read, i, rows, :], ahead)
+
+                @pl.when(ok)
+                def _(side=side):
+                    pair_copy(s + 1, side, both).start()
+
             full[plane(0), :] = whole(0)
             full[plane(CZ - 1), :] = whole(CZ - 1)
-            q_next = order[jnp.minimum(s + 1, SWEEPS - 1)]
-            read = jnp.where(q_next == q, 1, 0)
-            half_send[0] = folded(nxt[read, 1, rows, :], q_next)
-            half_send[1] = folded(nxt[read, PAIRS, rows, :], 1 - q_next)
-            start_halo(s + 1)
             start_far(s + 1)
 
         unless_last(send_outer)
@@ -446,7 +479,7 @@
             far_copy(s).wait_recv()
 
         near_ok = jnp.where(p == 0, has_dn, has_up)
-        zplanes[p] = jnp.where(near_ok, 4.0 * near_rx[s, p], 0.0)
+        zplanes[p] = jnp.where(near_ok, 4.0 * near[p], 0.0)
         zplanes[1 - p] = jnp.where(far_from_ok, 4.0 * far_rx[s], 0.0)
         for slot in range(SLOTS):
             now, new = patch_bufs[b], patch_bufs[1 - b]
@@ -458,19 +491,26 @@
                 def _(slot=slot, new=new):
                     live = slot < owned[p]
 
-                    def join(j, carry):
-                        one = 0.25 * new[slot, 0, j + 1, pl.ds(TOP, HALF), :]
-                        two = 0.25 * new[slot, 1, j + 1, pl.ds(TOP, HALF), :]
-                        for odd in range(2):
-                            z = pl.ds(odd, HALF, stride=2)
-                            swept = jnp.where(fine_parity == (q + odd) % 2, one, two)
-                            out_stage[slot, j, z, :] = jnp.where(live, swept, raw_pot[slot, j, z, :])
-                        pltpu.make_async_copy(
-                            out_stage.at[slot, j], patch_hbm.at[slot, :, columns(j)], out_sem.at[slot]
-                        ).start()
+                    def join(k, carry):
+                        joined = []
+                        for t in range(JOIN):
+                            j = k * JOIN + t
+                            one = 0.25 * new[slot, 0, j + 1, pl.ds(TOP, HALF), :]
+                            two = 0.25 * new[slot, 1, j + 1, pl.ds(TOP, HALF), :]
+                            for odd in range(2):
+                                old = raw_pot[slot, j, pl.ds(odd, HALF, stride=2), :]
+                                swept = jnp.where(fine_parity == (q + odd) % 2, one, two)
+                                joined.append((j, odd, jnp.where(live, swept, old)))
+                        for j, odd, cells in joined:
+                            out_stage[slot, j, pl.ds(odd, HALF, stride=2), :] = cells
+                        for t in range(JOIN):
+                            j = k * JOIN + t
+                            pltpu.make_async_copy(
+                                out_stage.at[slot, j], patch_hbm.at[slot, :, columns(j)], out_sem.at[slot]
+                            ).start()
                         return carry
 
-                    lax.fori_loop(0, HALF, join, 0)
+                    lax.fori_loop(0, HALF // JOIN, join, 0)
 
     def two_sweeps(t, carry):
         sweep(2 * t, 0, False)
@@ -504,9 +544,10 @@
             pltpu.VMEM((2, N + 2 * TOP, N), f32),
             pltpu.VMEM((2, PAIRS, N, N), f32),
             pltpu.VMEM((2, 2, N, N), f32),
+            pltpu.VMEM((2, N, N), f32),
+            pltpu.VMEM((2, N, N), f32),
+            pltpu.VMEM((2, N, N), f32),
             pltpu.VMEM((SWEEPS, 2, N, N), f32),
-            pltpu.VMEM((2, FINE, N), f32),
-            pltpu.VMEM((SWEEPS, 2, FINE, N), f32),
             pltpu.VMEM((2, 2, FINE, N), f32),
             pltpu.VMEM((2, 2, FINE, N), f32),
             pltpu.VMEM((CZ, N), f32),
@@ -526,7 +567,7 @@
             dma((CZ + 3,)),
             dma((SLOTS + 1,)),
             dma((2,)),
-            dma((SWEEPS, 2)),
+            dma((2,)),
             dma((2,)),
             dma((SWEEPS, 2)),
             dma((2, 2)),

time: 48.6 us -> 46.9 us (0.965); the launches traced: 48.4 us -> 46.2 us
  Pallas kernels: 45.6 us -> 43.4 us
    pallas_call x1, Pallas kernels: 45.6 us -> 43.4 us  [on_device(): pl.pallas_call(functools.partial(kernel, groups), out_shape=(pltpu.VMEM(p...]
where the time goes in v3:
time: 46.9 us; the launch traced here: 46.2 us
  Pallas kernels  43.4 us (93%)
  local copies, waits for them, and re-layouts  2.11 us (4%)
  between operations  0.64 us (1%)
    pallas_call x1, Pallas kernels, on_device(): pl.pallas_call(functools.partial(kernel, groups), out_shape=(pltpu.VMEM(p...  43.4 us
    unnamed x2, local copies, waits for them, and re-layouts  2.11 us

profile of v3, /device:TPU:6, one launch (start us, length us, event | category | flops | bytes accessed | tf_op | source)
XLA Modules:
  0.0 46.2 jit_solution(13438585120627505778)
XLA Ops:
  0.6 43.4 %smooth.1 = (f32[8,128,128]{2,1,0:T(8,128)S(1)}, f32[2,64,4096]{2,1,0:T(8,128)S(1)}) custom-call(s32[2,4]{1,0:T(2,128)} %bitcast.1, s32[2]{0:T(128)} %owned.1, s32[4]{0:T(128)} %order.1, f32[8,128,128]{2,1,0:T(8,128)} %phi_hbm.1, f32[8,128,128]{2,1,0:T(8,128)} %rho_hbm.1, f32[2,64,4096]{2,1,0:T(8,128)} %pot_hbm.1, f32[2,64,4096]{2,1,0:T(8,128)} %src_hbm.1), custom_call_target="tpu_custom_call" | custom-call | tf_op jit(solution)/shard_map/smooth/pallas_call | solution.py:532
  44.1 0.8 %copy.11 = f32[8,128,128]{2,1,0:T(8,128)} copy(f32[8,128,128]{2,1,0:T(8,128)S(1)} %get-tuple-element.2) | data formatting | bytes 1048576
  44.9 1.3 %copy.12 = f32[2,64,4096]{2,1,0:T(8,128)} copy(f32[2,64,4096]{2,1,0:T(8,128)S(1)} %get-tuple-element.3) | data formatting | bytes 4194304

commit v4 on v3

--- a/solution.py
+++ b/solution.py
@@ -19,7 +19,7 @@
 TOP = 8
 FULL = N + 8
 JOIN = 4
-JB = 8
+JB = 16
 
 
 def relaxed(center, neighbours, source):
@@ -305,7 +305,7 @@
             for t in range(JB):
                 below = other_ref[slot, role_b, j0 + t + 1, pl.ds(TOP - 1, HALF), :]
                 above = other_ref[slot, role_b, j0 + t + 1, pl.ds(TOP + 1, HALF), :]
-                face = x_face[k * (JB // 2) + t // 2]
+                face = x_face[slot, k * (JB // 2) + t // 2]
                 near = b[t + 1]
                 outs.append(
                     relaxed(
@@ -327,23 +327,33 @@
 
         lax.fori_loop(0, HALF // JB, step, 0)
 
-    def faces_of(s, slot, prev, nxt):
+    def set_faces(prev, nxt):
         data = pl.ds(TOP, HALF)
+        pitch = HALF + 2 * TOP
         w = 4.0 * w_rows[...]
-        for t in range(WIN):
-            low = jnp.broadcast_to(w[:, slot * FINE + t : slot * FINE + t + 1], (HALF, N))
-            high = jnp.broadcast_to(w[:, slot * FINE + WIN + t : slot * FINE + WIN + t + 1], (HALF, N))
-            x_face[t] = jnp.where(x_last, high, low)
-        y_face = split_dot(w, ey[slot])
-        oy = jnp.maximum(anchors[1, p * SLOTS + slot], 1)
-        z_rows = jnp.concatenate([zplanes[0, pl.ds(oy, WIN), :], zplanes[1, pl.ds(oy, WIN), :]], axis=0)
-        z_face = split_dot(z_rows, sx[slot])
-        for ref, role in ((prev, 0), (prev, 1), (nxt, 0)):
-            ref[slot, role, 0, data, :] = y_face
-            ref[slot, role, HALF + 1, data, :] = y_face
-            for j in range(HALF):
-                ref[slot, role, j + 1, TOP - 1 : TOP, :] = z_face[j // 2 : j // 2 + 1]
-                ref[slot, role, j + 1, TOP + HALF : TOP + HALF + 1, :] = z_face[WIN + j // 2 : WIN + j // 2 + 1]
+        y_faces, z_faces = [], []
+        for slot in range(SLOTS):
+            y_faces.append(split_dot(w, ey[slot]))
+            oy = jnp.maximum(anchors[1, p * SLOTS + slot], 1)
+            z_rows = jnp.concatenate([zplanes[0, pl.ds(oy, WIN), :], zplanes[1, pl.ds(oy, WIN), :]], axis=0)
+            z_faces.append(split_dot(z_rows, sx[slot]))
+        for slot in range(SLOTS):
+            for t in range(WIN):
+                at = slot * FINE + t
+                low = jnp.broadcast_to(w[:, at : at + 1], (HALF, N))
+                high = jnp.broadcast_to(w[:, at + WIN : at + WIN + 1], (HALF, N))
+                x_face[slot, t] = jnp.where(x_last, high, low)
+        for slot in range(SLOTS):
+            for ref, role in ((prev, 0), (prev, 1), (nxt, 0)):
+                ref[slot, role, 0, data, :] = y_faces[slot]
+                ref[slot, role, HALF + 1, data, :] = y_faces[slot]
+                lines = ref.reshape(SLOTS * 2 * (HALF + 2) * pitch, N)
+                start = (slot * 2 + role) * (HALF + 2) * pitch
+                for t in range(2):
+                    low = pl.ds(start + (t + 1) * pitch + TOP - 1, WIN, stride=2 * pitch)
+                    high = pl.ds(start + (t + 1) * pitch + TOP + HALF, WIN, stride=2 * pitch)
+                    lines[low, :] = z_faces[slot][:WIN]
+                    lines[high, :] = z_faces[slot][WIN:]
 
     patch_bufs = (pa, pb)
 
@@ -481,9 +491,9 @@
         near_ok = jnp.where(p == 0, has_dn, has_up)
         zplanes[p] = jnp.where(near_ok, 4.0 * near[p], 0.0)
         zplanes[1 - p] = jnp.where(far_from_ok, 4.0 * far_rx[s], 0.0)
+        now, new = patch_bufs[b], patch_bufs[1 - b]
+        set_faces(now, new)
         for slot in range(SLOTS):
-            now, new = patch_bufs[b], patch_bufs[1 - b]
-            faces_of(s, slot, now, new)
             patch_half(slot, now, first, now, 1 - first, new, 0, q)
             patch_half(slot, now, 1 - first, new, 0, new, 1, 1 - q)
             if may_end:
@@ -559,7 +569,7 @@
             pltpu.VMEM((SLOTS, 2, HALF + 2, HALF + 2 * TOP, N), f32),
             pltpu.VMEM((SLOTS, 2, HALF + 2, HALF + 2 * TOP, N), f32),
             pltpu.VMEM((SLOTS, 2, HALF, HALF, N), f32),
-            pltpu.VMEM((WIN, HALF, N), f32),
+            pltpu.VMEM((SLOTS, WIN, HALF, N), f32),
             pltpu.VMEM((SLOTS, N, N), bf16),
             pltpu.VMEM((SLOTS, N, N), bf16),
             pltpu.VMEM((CZ, N, N), f32),

time: 46.9 us -> 44.5 us (0.949); the launches traced: 46.2 us -> 44.3 us
  Pallas kernels: 43.4 us -> 41.5 us
    pallas_call x1, Pallas kernels: 43.4 us -> 41.5 us  [on_device(): pl.pallas_call(functools.partial(kernel, groups), out_shape=(pltpu.VMEM(p...]
where the time goes in v4:
time: 44.5 us; the launch traced here: 44.3 us
  Pallas kernels  41.5 us (93%)
  local copies, waits for them, and re-layouts  2.11 us (5%)
  between operations  0.64 us (1%)
    pallas_call x1, Pallas kernels, on_device(): pl.pallas_call(functools.partial(kernel, groups), out_shape=(pltpu.VMEM(p...  41.5 us
    unnamed x2, local copies, waits for them, and re-layouts  2.11 us

profile of v4, /device:TPU:6, one launch (start us, length us, event | category | flops | bytes accessed | tf_op | source)
XLA Modules:
  0.0 44.3 jit_solution(7763445349275077352)
XLA Ops:
  0.6 41.5 %smooth.1 = (f32[8,128,128]{2,1,0:T(8,128)S(1)}, f32[2,64,4096]{2,1,0:T(8,128)S(1)}) custom-call(s32[2,4]{1,0:T(2,128)} %bitcast.1, s32[2]{0:T(128)} %owned.1, s32[4]{0:T(128)} %order.1, f32[8,128,128]{2,1,0:T(8,128)} %phi_hbm.1, f32[8,128,128]{2,1,0:T(8,128)} %rho_hbm.1, f32[2,64,4096]{2,1,0:T(8,128)} %pot_hbm.1, f32[2,64,4096]{2,1,0:T(8,128)} %src_hbm.1), custom_call_target="tpu_custom_call" | custom-call | tf_op jit(solution)/shard_map/smooth/pallas_call | solution.py:542
  42.1 0.8 %copy.11 = f32[8,128,128]{2,1,0:T(8,128)} copy(f32[8,128,128]{2,1,0:T(8,128)S(1)} %get-tuple-element.2) | data formatting | bytes 1048576
  42.9 1.3 %copy.12 = f32[2,64,4096]{2,1,0:T(8,128)} copy(f32[2,64,4096]{2,1,0:T(8,128)S(1)} %get-tuple-element.3) | data formatting | bytes 4194304

commit v5 on v4

--- a/solution.py
+++ b/solution.py
@@ -19,7 +19,7 @@
 TOP = 8
 FULL = N + 8
 JOIN = 4
-JB = 16
+JB = 32
 
 
 def relaxed(center, neighbours, source):
@@ -190,7 +190,6 @@
     for which in range(2):
         rho_send[which, 0] = folded(raw_rho[0], (q_start + which) % 2)
         rho_send[which, 1] = folded(raw_rho[CZ - 1], (q_start + which + 1) % 2)
-    pack_faces()
 
     pl.semaphore_wait(barrier, sum(ok.astype(jnp.int32) for _, ok in greeted))
 
@@ -216,8 +215,9 @@
             pair_copy(0, side, second_only).start()
     start_rho(0)
     start_far(0)
+    start_rho(1)
+    pack_faces()
     w_copy(0).start()
-    start_rho(1)
     lax.fori_loop(0, HALF, fetch, 0)
 
     for i in range(PAIRS):
@@ -404,8 +404,7 @@
             def _(side=side):
                 halo[side, rows, :] = jnp.zeros((N, N), jnp.float32)
 
-        coarse_pairs(s, b, first, q, (1, PAIRS), True)
-        coarse_pairs(s, b, first, q, (0, PAIRS + 1), True)
+        coarse_pairs(s, b, first, q, (1, PAIRS, 0, PAIRS + 1), True)
         for side, ok in sides:
             @pl.when(jnp.logical_not(ok))
             def _(side=side):
@@ -493,12 +492,12 @@
         zplanes[1 - p] = jnp.where(far_from_ok, 4.0 * far_rx[s], 0.0)
         now, new = patch_bufs[b], patch_bufs[1 - b]
         set_faces(now, new)
-        for slot in range(SLOTS):
+        def sweep_slot(slot, carry):
             patch_half(slot, now, first, now, 1 - first, new, 0, q)
             patch_half(slot, now, 1 - first, new, 0, new, 1, 1 - q)
             if may_end:
                 @pl.when(s == SWEEPS - 1)
-                def _(slot=slot, new=new):
+                def _():
                     live = slot < owned[p]
 
                     def join(k, carry):
@@ -521,6 +520,9 @@
                         return carry
 
                     lax.fori_loop(0, HALF // JOIN, join, 0)
+            return carry
+
+        lax.fori_loop(0, SLOTS, sweep_slot, 0)
 
     def two_sweeps(t, carry):
         sweep(2 * t, 0, False)

time: 44.5 us -> 44.3 us (level)
  no operation moved by 1% of the time
where the time goes in v5:
time: 44.3 us; the launch traced here: 44.1 us
  Pallas kernels  41.3 us (93%)
  local copies, waits for them, and re-layouts  2.11 us (5%)
  between operations  0.64 us (1%)
    pallas_call x1, Pallas kernels, on_device(): pl.pallas_call(functools.partial(kernel, groups), out_shape=(pltpu.VMEM(p...  41.3 us
    unnamed x2, local copies, waits for them, and re-layouts  2.11 us

profile of v5, /device:TPU:6, one launch (start us, length us, event | category | flops | bytes accessed | tf_op | source)
XLA Modules:
  0.0 44.1 jit_solution(5252228286604067941)
XLA Ops:
  0.6 41.3 %smooth.1 = (f32[8,128,128]{2,1,0:T(8,128)S(1)}, f32[2,64,4096]{2,1,0:T(8,128)S(1)}) custom-call(s32[2,4]{1,0:T(2,128)} %bitcast.1, s32[2]{0:T(128)} %owned.1, s32[4]{0:T(128)} %order.1, f32[8,128,128]{2,1,0:T(8,128)} %phi_hbm.1, f32[8,128,128]{2,1,0:T(8,128)} %rho_hbm.1, f32[2,64,4096]{2,1,0:T(8,128)} %pot_hbm.1, f32[2,64,4096]{2,1,0:T(8,128)} %src_hbm.1), custom_call_target="tpu_custom_call" | custom-call | tf_op jit(solution)/shard_map/smooth/pallas_call | solution.py:544
  41.9 0.8 %copy.11 = f32[8,128,128]{2,1,0:T(8,128)} copy(f32[8,128,128]{2,1,0:T(8,128)S(1)} %get-tuple-element.2) | data formatting | bytes 1048576
  42.7 1.3 %copy.12 = f32[2,64,4096]{2,1,0:T(8,128)} copy(f32[2,64,4096]{2,1,0:T(8,128)S(1)} %get-tuple-element.3) | data formatting | bytes 4194304

commit v6 on v5

--- a/solution.py
+++ b/solution.py
@@ -18,7 +18,7 @@
 WIN = 16
 TOP = 8
 FULL = N + 8
-JOIN = 4
+JOIN = 8
 JB = 32
 
 

time: 44.3 us -> 44.3 us (level)
  no operation moved by 1% of the time
where the time goes in v6:
time: 44.3 us; the launch traced here: 44 us
  Pallas kernels  41.3 us (93%)
  local copies, waits for them, and re-layouts  2.11 us (5%)
  between operations  0.64 us (1%)
    pallas_call x1, Pallas kernels, on_device(): pl.pallas_call(functools.partial(kernel, groups), out_shape=(pltpu.VMEM(p...  41.3 us
    unnamed x2, local copies, waits for them, and re-layouts  2.11 us

profile of v6, /device:TPU:6, one launch (start us, length us, event | category | flops | bytes accessed | tf_op | source)
XLA Modules:
  0.0 44.0 jit_solution(14783065604203718192)
XLA Ops:
  0.6 41.3 %smooth.1 = (f32[8,128,128]{2,1,0:T(8,128)S(1)}, f32[2,64,4096]{2,1,0:T(8,128)S(1)}) custom-call(s32[2,4]{1,0:T(2,128)} %bitcast.1, s32[2]{0:T(128)} %owned.1, s32[4]{0:T(128)} %order.1, f32[8,128,128]{2,1,0:T(8,128)} %phi_hbm.1, f32[8,128,128]{2,1,0:T(8,128)} %rho_hbm.1, f32[2,64,4096]{2,1,0:T(8,128)} %pot_hbm.1, f32[2,64,4096]{2,1,0:T(8,128)} %src_hbm.1), custom_call_target="tpu_custom_call" | custom-call | tf_op jit(solution)/shard_map/smooth/pallas_call | solution.py:544
  41.9 0.8 %copy.11 = f32[8,128,128]{2,1,0:T(8,128)} copy(f32[8,128,128]{2,1,0:T(8,128)S(1)} %get-tuple-element.2) | data formatting | bytes 1048576
  42.7 1.3 %copy.12 = f32[2,64,4096]{2,1,0:T(8,128)} copy(f32[2,64,4096]{2,1,0:T(8,128)S(1)} %get-tuple-element.3) | data formatting | bytes 4194304
